TPU v7x, 512 devices: a whole 4x8x8 slice. The times are simulated.
512 devices in a mesh: seq: 128 (over z_hi, y, x, core), mp: 4 (over z_lo).
Axes of the slice: x: 4, y: 8, z: 8 (z_hi: 2, z_lo: 4; z = z_hi * 4 + z_lo), core: 2. Of those that a mesh axis runs over, the one named last changes fastest.
Arguments:
- coarse: bfloat16 [768, 16384], P('mp', 'seq'), may hold values from -6 to 6
- skip: bfloat16 [768, 32768], P('mp', 'seq'), may hold values from -6 to 6
- conv_weight: bfloat16 [3, 768, 768], P(None, 'mp'), may hold values from -0.125 to 0.125
- conv_bias: float32 [768], P('mp'), may hold values from -3 to 3
- head_weight: bfloat16 [768, 512], P(None, 'mp'), may hold values from -0.21875 to 0.21875
- head_bias: float32 [512], P('mp'), may hold values from -3 to 3
- counts: int32 [32768, 512], P('seq', 'mp'), may hold values from 0 to 3
- seg_mask: int32 [16, 512], P(None, 'mp'), may hold values 0 or 1
Outputs:
- grad_skip: bfloat16 [768, 32768], P('mp', 'seq')
- grad_coarse: bfloat16 [768, 16384], P('mp', 'seq')
- grad_head: float32 [768, 512], P('seq', 'mp')
- grad_conv: float32 [768, 3, 768], P('seq', None, 'mp')
All inputs are finite; a program needn't handle non-finite values. No bound on the sum of `seg_mask` on one device may be relied on, other than what follows from the above.
Results may differ from a plain program's by a relative error of at most 0.0068.
Values may be sent and summed in bfloat16 or wider, within the bound.
A program may use at most 64 MiB of HBM per device.

v0:
```python
import math

import jax
import jax.numpy as jnp
from jax import lax
from jax.sharding import PartitionSpec as P

root_two_pi = 0.7978845608028654
cubic_coef = 0.044715
multi_weight = 5.0
pseudo_count = 0.5


def extended(block, sides, width):
    for axis, dim in sides:
        count = lax.axis_size(axis)
        forward = [(i, i + 1) for i in range(count - 1)]
        backward = [(target, source) for source, target in forward]
        low = lax.ppermute(
            lax.slice_in_dim(block, block.shape[dim] - width, None, axis=dim), axis, forward
        )
        high = lax.ppermute(lax.slice_in_dim(block, 0, width, axis=dim), axis, backward)
        block = jnp.concatenate([low, block, high], axis=dim)
    return block


def gelu_value(inputs):
    inner = root_two_pi * (inputs + cubic_coef * inputs * inputs * inputs)
    return 0.5 * inputs * (1.0 + jnp.tanh(inner))


def gelu_slope(inputs):
    inner = root_two_pi * (inputs + cubic_coef * inputs * inputs * inputs)
    tangent = jnp.tanh(inner)
    return 0.5 * (1.0 + tangent) + 0.5 * inputs * (1.0 - tangent * tangent) * root_two_pi * (
        1.0 + 3.0 * cubic_coef * inputs * inputs
    )


def contract_first(left, right):
    return lax.dot_general(
        left, right, (((0,), (0,)), ((), ())), preferred_element_type=jnp.float32
    )


def contract_last(left, right):
    return lax.dot_general(
        left, right, (((1,), (1,)), ((), ())), preferred_element_type=jnp.float32
    )


def shards(coarse, skip, conv_weight, conv_bias, head_weight, head_bias, counts, seg_mask):
    width_dev = skip.shape[0]
    length_dev = skip.shape[1]
    taps = conv_weight.shape[0]
    reach = taps // 2
    seq_count = lax.axis_size("seq")
    scale_back = 1.0 / math.sqrt(length_dev * seq_count)
    doubled = jnp.repeat(coarse.astype(jnp.float32), 2, axis=1)
    summed = (doubled + skip.astype(jnp.float32)).astype(jnp.bfloat16)
    padded = extended(summed, (("seq", 1),), reach)
    widened = lax.all_gather(padded, "mp", axis=0, tiled=True)
    conv_out = jnp.zeros((width_dev, length_dev), jnp.float32)
    for offset in range(taps):
        conv_out = conv_out + jnp.dot(
            conv_weight[offset],
            widened[:, offset : offset + length_dev],
            preferred_element_type=jnp.float32,
        )
    before = conv_out + conv_bias[:, None]
    hidden = (summed.astype(jnp.float32) + gelu_value(before)).astype(jnp.bfloat16)
    hidden_full = lax.all_gather(hidden, "mp", axis=0, tiled=True)
    logits = contract_first(hidden_full, head_weight) + head_bias
    predicted = jax.nn.softplus(logits) + pseudo_count
    observed = counts.astype(jnp.float32)
    pred_sum = jnp.sum(predicted, axis=0)
    count_sum = jnp.sum(observed, axis=0)
    span = min(8, seq_count)
    position = lax.axis_index("seq")
    segment = position // span
    seg_count = seq_count // span
    member = (jnp.arange(seg_count, dtype=jnp.int32) == segment).astype(jnp.float32)[:, None]
    pred_table, count_table = lax.psum(
        (member * pred_sum[None, :], member * count_sum[None, :]), "seq"
    )
    pred_total = jnp.sum(member * pred_table, axis=0)
    count_total = jnp.sum(member * count_table, axis=0)
    mask_row = lax.dynamic_slice_in_dim(seg_mask, segment, 1, 0).astype(jnp.float32)
    slope_pred = mask_row * (
        1.0 + (multi_weight - 1.0) * count_total / pred_total - multi_weight * observed / predicted
    )
    grad_logits = (slope_pred * jax.nn.sigmoid(logits)).astype(jnp.bfloat16)
    track_full = lax.all_gather(grad_logits, "mp", axis=1, tiled=True)
    head_own = lax.all_to_all(head_weight, "mp", split_axis=0, concat_axis=1, tiled=True)
    grad_hidden = contract_last(head_own, track_full)
    grad_head = (
        lax.psum_scatter(
            jnp.dot(hidden_full, grad_logits, preferred_element_type=jnp.float32),
            "seq",
            scatter_dimension=0,
            tiled=True,
        )
        * scale_back
    )
    grad_before = (grad_hidden * gelu_slope(before)).astype(jnp.bfloat16)
    grad_padded = extended(grad_before, (("seq", 1),), reach)
    every_weight = lax.all_gather(conv_weight, "mp", axis=1, tiled=True)
    weight_rows = lax.dynamic_slice_in_dim(
        every_weight, lax.axis_index("mp") * width_dev, width_dev, 2
    )
    carry = jnp.zeros((width_dev, length_dev), jnp.float32)
    piece = lax.all_gather(grad_padded, "mp", axis=0, tiled=True)
    for offset in range(taps):
        first_row = 2 * reach - offset
        block = weight_rows[offset]
        carry = carry + contract_first(block, piece[:, first_row : first_row + length_dev])
    grad_input = grad_hidden + carry
    grad_skip = grad_input.astype(jnp.bfloat16)
    grad_coarse = jnp.sum(grad_input.reshape(width_dev, length_dev // 2, 2), axis=2).astype(
        jnp.bfloat16
    )
    grad_conv = (
        lax.psum_scatter(
            jnp.stack(
                [
                    contract_last(widened[:, offset : offset + length_dev], grad_before)
                    for offset in range(taps)
                ],
                axis=1,
            ),
            "seq",
            scatter_dimension=0,
            tiled=True,
        )
        * scale_back
    )
    return (grad_skip, grad_coarse, grad_head, grad_conv)


def solution(mesh):
    in_specs = (
        P("mp", "seq"),
        P("mp", "seq"),
        P(None, "mp", None),
        P("mp"),
        P(None, "mp"),
        P("mp"),
        P("seq", "mp"),
        P(None, "mp"),
    )
    out_specs = (P("mp", "seq"), P("mp", "seq"), P("seq", "mp"), P("seq", None, "mp"))
    return jax.shard_map(shards, mesh=mesh, in_specs=in_specs, out_specs=out_specs, check_vma=False)
```

profile of v0, /device:TPU:1, one launch (start us, length us, event | category | flops | bytes accessed | tf_op | source)
XLA Modules:
  0.0 2439.0 jit_solution(10214006406482186566)
XLA Ops:
  8.0 1.0 copy.36
  9.4 0.9 add_convert_fusion.1
  10.4 8.8 collective-permute-start.1
  19.2 1.9 collective-permute-start
  21.1 3.4 all-to-all-start
  24.6 1.0 convert_reduce_fusion
  25.6 0.7 fusion.35
  26.5 14.5 all-gather
  41.2 0.5 reshape.36
  41.8 0.3 fusion.12
  42.1 0.3 convolution_add_fusion.3
  42.4 0.4 add_convert_fusion
  42.8 11.5 all_gather.16
  54.3 0.4 fusion.30
  54.7 796.7 %all-reduce.2 = (f32[16,128]{1,0:T(8,128)S(1)}, f32[16,128]{1,0:T(8,128)S(1)}) all-reduce(f32[16,128]{1,0:T(8,128)S(1)} %get-tuple-element.35, f32[16,128]{1,0:T(8,128)S(1)} %get-tuple-element.34), channel_id=1, replica_groups=mesh['seq'=128,'mp'=4] {'seq'}, use_global_device_ids=true, to_apply=%region_1.2 | all-reduce | flops 4096 | bytes 32768 | tf_op jit(solution)/shard_map/psum | solution.py:83
  851.7 10.5 all_gather.17
  862.2 1.0 fusion.40
  864.4 2.8 copy.44
  867.3 0.5 all-gather.4.cloned.1.call-update
  867.9 14.4 collective-permute-start.3
  882.3 1.9 collective-permute-start.2
  884.2 1.3 dynamic-slice
  886.4 12.9 all-gather.1
  899.5 0.5 reshape.38
  900.1 1522.0 %all-reduce.6.cloned.1.call-done = (f32[768,128]{1,0:T(8,128)}, f32[768,3,192]{2,1,0:T(4,128)}) async-done(((f32[768,128]{1,0:T(8,128)}, f32[768,3,192]{2,1,0:T(4,128)}), (f32[768,128]{1,0:T(8,128)}, f32[768,3,192]{2,1,0:T(4,128)})) %all-reduce.6.cloned.1.call-update) | async-done | bytes 2162704
  2422.1 1.3 dynamic-slice_multiply_fusion.1
  2423.4 1.4 dynamic-slice_multiply_fusion
  2424.8 1.6 fusion.5
  2426.4 1.6 convolution_add_fusion.1
  2428.0 2.2 fusion.39
  2430.5 0.3 reduce_sum.49
  2430.8 0.7 copy.45
  (42 shorter events, 3.3 us)
Async XLA Ops:
  8.0 33.8 %copy-start = (bf16[3,192,768]{2,1,0:T(8,128)(2,1)S(1)}, bf16[3,192,768]{2,1,0:T(8,128)(2,1)}, u32[]{:S(2)}) copy-start(bf16[3,192,768]{2,1,0:T(8,128)(2,1)} %param.10) | copy-start | bytes 2654212
  10.3 32.1 %copy-start.3 = (f32[192]{0:T(256)S(1)}, f32[192]{0:T(256)}, u32[]{:S(2)}) copy-start(f32[192]{0:T(256)} %param.11) | copy-start | bytes 2308
  10.4 15.8 collective-permute-start.1
  19.2 7.1 collective-permute-start
  21.1 842.1 %all-to-all-start = ((bf16[4,192,128]{2,1,0:T(8,128)(2,1)}), bf16[4,192,128]{2,1,0:T(8,128)(2,1)S(1)}, u32[]{:S(2)}, u32[]{:S(2)}) async-start(bf16[4,192,128]{2,1,0:T(8,128)(2,1)} %bitcast.66), calls=%async_computation | async-start | bytes 393216 | tf_op jit(solution)/shard_map/all_to_all | solution.py:94
  24.5 2397.6 %all-reduce.6.cloned.1.call-start = ((), (), s32[]{:S(2)}) async-start(), calls=%async_computation.2 | async-start | bytes 7077888
  41.0 13.3 copy-start.2
  41.0 13.3 copy-start.4
  41.2 810.3 %copy-start.1 = (s32[256,128]{1,0:T(8,128)S(1)}, s32[256,128]{1,0:T(8,128)}, u32[]{:S(2)}) copy-start(s32[256,128]{1,0:T(8,128)} %param.14) | copy-start | bytes 393220
  867.2 1557.6 %all-gather.4.cloned.1.call-start = ((), (), s32[]{:S(2)}) async-start(), calls=%async_computation.1 | async-start | bytes 4423680 | tf_op jit(solution)/shard_map/all_gather | solution.py:107
  867.9 18.2 collective-permute-start.3
  882.3 3.9 collective-permute-start.2
Sparse Core Ops, SparseCore 0:
  867.3 1554.7 all-reduce.5
Sparse Core Ops, SparseCore 1:
  869.8 87.8 all-gather.3
where the time goes:
time: 2440 us
  waiting for transfers between devices  1520 us (62%)
  blocking collectives  846 us (35%)
  starting transfers between devices  30.5 us (1%)
    unnamed x3, waiting for transfers between devices  1520 us
    psum x1, blocking collectives, shards(): lax.psum((member * pred_sum[None, :], member * count_sum[None, :]), 'seq')  797 us
  transfers between devices with their start and end apart: 7, of which 1 were waited for; matrix products, arithmetic and copies ran while one was open for 0% of the time, Pallas kernels for 0%

commit v1 on v0

v1 whole, which is shorter than its diff:
```python
import functools
import math

import jax
import jax.numpy as jnp
from jax import lax
from jax.experimental import pallas as pl
from jax.experimental.pallas import tpu as pltpu
from jax.sharding import PartitionSpec as P

root_two_pi = 0.7978845608028654
cubic_coef = 0.044715
multi_weight = 5.0
pseudo_count = 0.5

CORES, XS, YS, HIS, MPS = 2, 4, 8, 2, 4
ROW = XS * CORES
SEQ = HIS * YS * ROW

F32 = jnp.float32
BF16 = jnp.bfloat16


def gelu_parts(v):
    tangent = jnp.tanh(root_two_pi * (v + cubic_coef * v * v * v))
    value = 0.5 * v * (1.0 + tangent)
    slope = 0.5 * (1.0 + tangent) + 0.5 * v * (1.0 - tangent * tangent) * root_two_pi * (
        1.0 + 3.0 * cubic_coef * v * v
    )
    return value, slope


def dot(left, right, dims):
    return lax.dot_general(left, right, (dims, ((), ())), preferred_element_type=F32)


NN = ((1,), (0,))
NT = ((1,), (1,))
TN = ((0,), (0,))


def iota(shape, axis):
    return lax.broadcasted_iota(jnp.int32, shape, axis)


def one_hot(mask):
    return jnp.where(mask, 1.0, 0.0).astype(BF16)


def body(
    coarse, skip, weight, conv_bias, head, head_bias, counts, seg_mask,
    out_skip, out_coarse, out_head, out_conv,
    summed_all, edge_in, edge_all, hidden_all, head_own, track_all, seg_all,
    before_ref, slope_ref, grad_hidden_ref, gb_ref, gedge, shifted,
    pick, summed_pick, hidden_pick, turned,
    back_send, back_recv, own_half, core_send, core_recv,
    x_send, x_recv, y_send, y_recv, hi_send, hi_recv,
    edge_sems, sum_sems, rows_sems, hid_sems, head_sems, seg_sems, track_sems,
    gedge_sems, back_sems, core_sems, x_sems, y_sems, hi_sems,
):
    width, length = skip.shape
    half = length // 2
    channels = head.shape[0]
    tracks = head.shape[1]
    unit = channels // SEQ
    cols = core_send.shape[1]
    conv_cols = 3 * width
    scale_back = 1.0 / math.sqrt(length * SEQ)

    s = lax.axis_index("seq")
    z = lax.axis_index("mp")
    core = lax.rem(s, CORES)
    x = lax.rem(s // CORES, XS)
    y = lax.rem(s // ROW, YS)
    hi = s // (ROW * YS)

    mp_peer = [lax.rem(z + d, MPS) for d in range(MPS)]
    row_base = s - lax.rem(s, ROW)
    row_peer = [row_base + lax.rem(lax.rem(s, ROW) + d, ROW) for d in range(ROW)]
    core_peer = s + 1 - 2 * core
    x_peer = [s + CORES * (lax.rem(x + d, XS) - x) for d in range(XS)]
    y_peer = [s + ROW * (lax.rem(y + d, YS) - y) for d in range(YS)]
    hi_peer = s + ROW * YS * (1 - 2 * hi)
    right = lax.rem(s + 1, SEQ)
    left = lax.rem(s + SEQ - 1, SEQ)

    def send(src, dst, sems, slot, device):
        copy = pltpu.make_async_remote_copy(
            src_ref=src,
            dst_ref=dst,
            send_sem=sems.at[0, slot],
            recv_sem=sems.at[1, slot],
            device_id=device,
            device_id_type=pl.DeviceIdType.MESH,
        )
        copy.start()
        return copy

    barrier = pltpu.get_barrier_semaphore()
    greeted = [{"mp": p} for p in mp_peer[1:]]
    greeted += [{"seq": p} for p in row_peer[1:] + y_peer[1:] + [hi_peer, left, right]]
    for device in greeted:
        pl.semaphore_signal(barrier, inc=1, device_id=device, device_id_type=pl.DeviceIdType.MESH)

    spread = one_hot(iota((half, length), 1) // 2 == iota((half, length), 0))
    doubled = dot(coarse[...], spread, NN)
    summed = (doubled + skip[...].astype(F32)).astype(BF16)
    summed_all[z] = summed

    pl.semaphore_wait(barrier, len(greeted))

    edge_copies = [
        send(summed_all.at[z, :, pl.ds(half, half)], edge_in.at[0], edge_sems, 0, {"seq": right}),
        send(summed_all.at[z, :, pl.ds(0, half)], edge_in.at[1], edge_sems, 1, {"seq": left}),
    ]
    sum_copies = [
        send(summed_all.at[z], summed_all.at[z], sum_sems, d - 1, {"mp": mp_peer[d]})
        for d in range(1, MPS)
    ]

    group = channels // ROW
    row = iota((group, channels), 0)
    lane = iota((group, channels), 1)
    step = HIS * unit
    y_step = jnp.zeros_like(row)
    for j in range(1, YS):
        y_step = y_step + jnp.where(row >= step * j, 1, 0)
    rest = row - step * y_step
    hi_step = jnp.where(rest >= unit, 1, 0)
    rest = rest - unit * hi_step
    y_at = y + y_step
    y_at = jnp.where(y_at >= YS, y_at - YS, y_at)
    hi_at = jnp.where(hi_step == 1, 1 - hi, hi)
    base = ((hi_at * YS + y_at) * ROW) * unit + rest
    for c in range(CORES):
        core_at = core if c == 0 else 1 - core
        for d in range(XS):
            x_at = lax.rem(x + d, XS)
            place = (c * XS + d) * group
            pick[place : place + group, :] = one_hot(
                lane == base + (x_at * CORES + core_at) * unit
            )

    for k in range(3):
        turned[k] = weight[k].T

    for copy in edge_copies:
        copy.wait()
    first = jnp.where(s == 0, 0.0, 1.0).astype(BF16)
    last = jnp.where(s == SEQ - 1, 0.0, 1.0).astype(BF16)
    shape = (16, half)
    low_row = one_hot((iota(shape, 0) == 0) & (iota(shape, 1) == half - 1)) * first
    high_row = one_hot((iota(shape, 0) == 1) & (iota(shape, 1) == 0)) * last
    rows = dot(low_row, edge_in[0], NT) + dot(high_row, edge_in[1], NT)
    edge_all[z] = jnp.zeros((16, edge_all.shape[2]), BF16)
    edge_all[z, :, 0:width] = rows.astype(BF16)
    rows_copies = [
        send(edge_all.at[z], edge_all.at[z], rows_sems, d - 1, {"mp": mp_peer[d]})
        for d in range(1, MPS)
    ]

    for copy in sum_copies:
        copy.wait()
    head_copies = [
        send(
            head.at[pl.ds(pl.multiple_of(mp_peer[d] * width, width), width), :],
            head_own.at[z],
            head_sems,
            d - 1,
            {"mp": mp_peer[d]},
        )
        for d in range(1, MPS)
    ]
    head_own[z] = head[pl.ds(pl.multiple_of(z * width, width), width), :]
    summed_full = summed_all[...].reshape(channels, length)
    bias_rows = jnp.zeros((16, width), F32)
    bias = conv_bias[...]
    part0 = bias.astype(BF16).astype(F32)
    part1 = (bias - part0).astype(BF16).astype(F32)
    part2 = bias - part0 - part1
    at = iota((16, width), 0)
    bias_rows = jnp.where(at == 0, part0, jnp.where(at == 1, part1, jnp.where(at == 2, part2, 0.0)))
    before = dot(bias_rows.astype(BF16), jnp.ones((16, length), BF16), TN)
    before = before + dot(weight[1], summed_full, NN)
    from_low = dot(weight[0], summed_full, NN)
    from_high = dot(weight[2], summed_full, NN)

    for copy in rows_copies:
        copy.wait()
    edges = jnp.zeros((16, channels), F32)
    span = edge_all.shape[2]
    for k in range(MPS):
        placed = one_hot(
            (iota((span, channels), 1) == iota((span, channels), 0) + k * width)
            & (iota((span, channels), 0) < width)
        )
        edges = edges + dot(edge_all[k], placed, NN)
    edges = edges.astype(BF16)
    low_col = dot(weight[0], edges, NT)[:, 0:1]
    high_col = dot(weight[2], edges, NT)[:, 1:2]
    lanes = iota((width, length), 1)
    before = before + jnp.where(lanes == 0, low_col, pltpu.roll(from_low, 1, 1))
    before = before + jnp.where(lanes == length - 1, high_col, pltpu.roll(from_high, length - 1, 1))
    value, slope = gelu_parts(before)
    hidden_all[z] = (summed_all[z].astype(F32) + value).astype(BF16)
    hidden_copies = [
        send(hidden_all.at[z], hidden_all.at[z], hid_sems, d - 1, {"mp": mp_peer[d]})
        for d in range(1, MPS)
    ]
    slope_ref[...] = slope
    summed_pick[...] = dot(pick[...], summed_full, NN).astype(BF16)
    observed = counts[...].astype(F32)
    mine = lax.rem(s, ROW)
    seg_all[mine] = jnp.zeros(seg_all.shape[1:], F32)
    seg_all[mine, 1:2, :] = jnp.sum(observed, axis=0, keepdims=True)

    for copy in hidden_copies:
        copy.wait()
    hidden_full = hidden_all[...].reshape(channels, length)
    logits = dot(hidden_full, head[...], TN) + head_bias[...]
    small = jnp.exp(-jnp.abs(logits))
    predicted = jnp.maximum(logits, 0.0) + jnp.log1p(small) + pseudo_count
    seg_all[mine, 0:1, :] = jnp.sum(predicted, axis=0, keepdims=True)
    seg_copies = [
        send(seg_all.at[mine], seg_all.at[mine], seg_sems, d - 1, {"seq": row_peer[d]})
        for d in range(1, ROW)
    ]
    hidden_pick[...] = dot(pick[...], hidden_full, NN).astype(BF16)
    sigmoid = jnp.where(logits >= 0.0, 1.0, small) / (1.0 + small)
    ratio = multi_weight * observed / predicted
    mask_row = seg_mask[pl.ds(s // ROW, 1), :].astype(F32)
    for copy in seg_copies:
        copy.wait()
    totals = seg_all[0]
    for k in range(1, ROW):
        totals = totals + seg_all[k]
    share = 1.0 + (multi_weight - 1.0) * totals[1:2, :] / totals[0:1, :]
    grad_logits = (mask_row * (share - ratio) * sigmoid).astype(BF16)
    track_all[z] = grad_logits
    track_copies = [
        send(track_all.at[z], track_all.at[z], track_sems, d - 1, {"mp": mp_peer[d]})
        for d in range(1, MPS)
    ]
    grad_head = dot(hidden_pick[...], grad_logits, NN)
    own_half[:, cols - tracks : cols] = grad_head[: channels // 2]
    core_send[:, cols - tracks : cols] = grad_head[channels // 2 :].astype(BF16)

    for copy in head_copies:
        copy.wait()
    for copy in track_copies:
        copy.wait()
    grad_hidden = dot(head_own[0], track_all[0], NT)
    for k in range(1, MPS):
        grad_hidden = grad_hidden + dot(head_own[k], track_all[k], NT)
    gb = (grad_hidden * slope_ref[...]).astype(BF16)
    gb_ref[...] = gb
    gedge_copies = [
        send(gb_ref.at[:, pl.ds(half, half)], gedge.at[0], gedge_sems, 0, {"seq": right}),
        send(gb_ref.at[:, pl.ds(0, half)], gedge.at[1], gedge_sems, 1, {"seq": left}),
    ]
    grad_hidden_ref[...] = grad_hidden
    shifted[width : 2 * width, :] = gb
    gb_wide = gb.astype(F32)
    to_left = pltpu.roll(gb_wide, length - 1, 1)
    to_right = pltpu.roll(gb_wide, 1, 1)
    for copy in gedge_copies:
        copy.wait()
    keep_low = jnp.where(s == 0, 0.0, 1.0)
    keep_high = jnp.where(s == SEQ - 1, 0.0, 1.0)
    low_col = gedge[0].astype(F32)[:, half - 1 : half] * keep_low
    high_col = gedge[1].astype(F32)[:, 0:1] * keep_high
    shifted[0:width, :] = jnp.where(lanes == length - 1, high_col, to_left).astype(BF16)
    shifted[2 * width :, :] = jnp.where(lanes == 0, low_col, to_right).astype(BF16)

    for k in range(ROW // 2, ROW):
        part = dot(summed_pick[k * group : (k + 1) * group, :], shifted[...], NT)
        at = (k - ROW // 2) * group
        core_send[at : at + group, 0:conv_cols] = part.astype(BF16)
        core_send[at : at + group, conv_cols : cols - tracks] = jnp.zeros(
            (group, cols - tracks - conv_cols), BF16
        )
    core_copy = send(core_send, core_recv, core_sems, 0, {"seq": core_peer})

    for d in (2, 1, 3, 0):
        at = pl.ds(pl.multiple_of(mp_peer[d] * width, width), width)
        total = jnp.zeros((width, length), F32)
        for k in range(3):
            total = total + dot(turned[k, at, :], shifted[k * width : (k + 1) * width, :], NN)
        if d == 0:
            grad_hidden_ref[...] += total
        else:
            back_send[d - 1] = total.astype(BF16)
    back_copies = [
        send(back_send.at[d - 1], back_recv.at[d - 1], back_sems, d - 1, {"mp": mp_peer[d]})
        for d in range(1, MPS)
    ]

    for k in range(ROW // 2):
        part = dot(summed_pick[k * group : (k + 1) * group, :], shifted[...], NT)
        at = k * group
        own_half[at : at + group, 0:conv_cols] = part
        own_half[at : at + group, conv_cols : cols - tracks] = jnp.zeros(
            (group, cols - tracks - conv_cols), F32
        )
    core_copy.wait()
    for d in range(1, XS):
        at = d * group
        x_send[d - 1] = (
            own_half[at : at + group, :] + core_recv[at : at + group, :].astype(F32)
        ).astype(BF16)
    x_copies = [
        send(x_send.at[d - 1], x_recv.at[d - 1], x_sems, d - 1, {"seq": x_peer[d]})
        for d in range(1, XS)
    ]
    total = own_half[0:group, :] + core_recv[0:group, :].astype(F32)
    for copy in x_copies:
        copy.wait()
    for d in range(1, XS):
        total = total + x_recv[d - 1].astype(F32)
    own_half[0:group, :] = total
    for d in range(1, YS):
        y_send[d - 1, 0:step, :] = own_half[d * step : (d + 1) * step, :].astype(BF16)
        y_send[d - 1, step:16, :] = jnp.zeros((16 - step, cols), BF16)
    y_copies = [
        send(y_send.at[d - 1], y_recv.at[d - 1], y_sems, d - 1, {"seq": y_peer[d]})
        for d in range(1, YS)
    ]

    for copy in back_copies:
        copy.wait()
    total = grad_hidden_ref[...]
    for d in range(1, MPS):
        total = total + back_recv[d - 1].astype(F32)
    out_skip[...] = total.astype(BF16)
    high = total.astype(BF16)
    rest = total - high.astype(F32)
    mid = rest.astype(BF16)
    low = (rest - mid.astype(F32)).astype(BF16)
    pairs = dot(high, spread, NT) + dot(mid, spread, NT) + dot(low, spread, NT)
    out_coarse[...] = pairs.astype(BF16)

    for copy in y_copies:
        copy.wait()
    total = own_half[0:16, :]
    for d in range(1, YS):
        total = total + y_recv[d - 1].astype(F32)
    hi_send[...] = total.astype(BF16)
    hi_copy = send(hi_send, hi_recv, hi_sems, 0, {"seq": hi_peer})
    hi_copy.wait()
    final = (total[0:unit, :] + hi_recv[...].astype(F32)[unit : 2 * unit, :]) * scale_back
    out_head[...] = final[:, cols - tracks :]
    for k in range(3):
        out_conv[:, k, :] = final[:, k * width : (k + 1) * width]


def shards(coarse, skip, conv_weight, conv_bias, head_weight, head_bias, counts, seg_mask):
    width, length = skip.shape
    channels, tracks = head_weight.shape
    half = length // 2
    group = channels // ROW
    cols = -(-3 * width // 128) * 128 + tracks
    unit = channels // SEQ
    wide = -(-width // 128) * 128

    def sems(count):
        return pltpu.SemaphoreType.DMA((2, count))

    scratch = [
        pltpu.VMEM((MPS, width, length), BF16),
        pltpu.VMEM((2, width, half), BF16),
        pltpu.VMEM((MPS, 16, wide), BF16),
        pltpu.VMEM((MPS, width, length), BF16),
        pltpu.VMEM((MPS, width, tracks), BF16),
        pltpu.VMEM((MPS, length, tracks), BF16),
        pltpu.VMEM((ROW, 8, tracks), F32),
        pltpu.VMEM((width, length), F32),
        pltpu.VMEM((width, length), F32),
        pltpu.VMEM((width, length), F32),
        pltpu.VMEM((width, length), BF16),
        pltpu.VMEM((2, width, half), BF16),
        pltpu.VMEM((3 * width, length), BF16),
        pltpu.VMEM((channels, channels), BF16),
        pltpu.VMEM((channels, length), BF16),
        pltpu.VMEM((channels, length), BF16),
        pltpu.VMEM((3, channels, width), BF16),
        pltpu.VMEM((MPS - 1, width, length), BF16),
        pltpu.VMEM((MPS - 1, width, length), BF16),
        pltpu.VMEM((channels // 2, cols), F32),
        pltpu.VMEM((channels // 2, cols), BF16),
        pltpu.VMEM((channels // 2, cols), BF16),
        pltpu.VMEM((XS - 1, group, cols), BF16),
        pltpu.VMEM((XS - 1, group, cols), BF16),
        pltpu.VMEM((YS - 1, 16, cols), BF16),
        pltpu.VMEM((YS - 1, 16, cols), BF16),
        pltpu.VMEM((16, cols), BF16),
        pltpu.VMEM((16, cols), BF16),
        sems(2), sems(MPS - 1), sems(MPS - 1), sems(MPS - 1), sems(MPS - 1), sems(ROW - 1),
        sems(MPS - 1), sems(2), sems(MPS - 1), sems(1), sems(XS - 1), sems(YS - 1), sems(1),
    ]
    vmem = pl.BlockSpec(memory_space=pltpu.VMEM)
    return pl.pallas_call(
        body,
        out_shape=(
            jax.ShapeDtypeStruct((width, length), BF16),
            jax.ShapeDtypeStruct((width, half), BF16),
            jax.ShapeDtypeStruct((unit, tracks), F32),
            jax.ShapeDtypeStruct((unit, 3, width), F32),
        ),
        in_specs=[vmem] * 8,
        out_specs=(vmem,) * 4,
        scratch_shapes=scratch,
        compiler_params=pltpu.CompilerParams(
            collective_id=0, has_side_effects=True, vmem_limit_bytes=48 * 1024 * 1024
        ),
    )(
        coarse, skip, conv_weight, conv_bias.reshape(1, -1), head_weight,
        head_bias.reshape(1, -1), counts, seg_mask,
    )


def solution(mesh):
    in_specs = (
        P("mp", "seq"),
        P("mp", "seq"),
        P(None, "mp", None),
        P("mp"),
        P(None, "mp"),
        P("mp"),
        P("seq", "mp"),
        P(None, "mp"),
    )
    out_specs = (P("mp", "seq"), P("mp", "seq"), P("seq", "mp"), P("seq", None, "mp"))
    return jax.shard_map(shards, mesh=mesh, in_specs=in_specs, out_specs=out_specs, check_vma=False)
```

time: 2440 us -> 85.1 us (0.03)
  the two profiles are of different devices: /device:TPU:1 before, /device:TPU:16 now
where the time goes in v1:
time: 85.1 us; the launch traced here: 84.8 us
  Pallas kernels  75.6 us (89%)
  local copies, waits for them, and re-layouts  8.51 us (10%)
    pallas_call x1, Pallas kernels, shards(): pl.pallas_call(body, out_shape=(jax.ShapeDtypeStruct((width, length), BF1...  75.6 us
    unnamed x20, local copies, waits for them, and re-layouts  8.51 us

profile of v1, /device:TPU:16, one launch (start us, length us, event | category | flops | bytes accessed | tf_op | source)
XLA Modules:
  0.0 84.8 jit_solution(5549308684078792299)
XLA Ops:
  0.6 0.0 copy-start.6
  0.6 0.0 copy-start.7
  0.7 0.7 copy-done.6
  1.3 0.0 copy-done.7
  1.3 0.0 copy-start
  1.3 1.2 %copy-done = bf16[3,192,768]{2,1,0:T(8,128)(2,1)S(1)} copy-done((bf16[3,192,768]{2,1,0:T(8,128)(2,1)S(1)}, bf16[3,192,768]{2,1,0:T(8,128)(2,1)}, u32[]{:S(2)}) %copy-start) | copy-done | bytes 884760
  2.5 0.0 copy-start.1
  2.5 0.9 %copy-done.1 = bf16[768,128]{1,0:T(8,128)(2,1)S(1)} copy-done((bf16[768,128]{1,0:T(8,128)(2,1)S(1)}, bf16[768,128]{1,0:T(8,128)(2,1)}, u32[]{:S(2)}) %copy-start.1) | copy-done | bytes 196632
  3.4 0.0 copy-start.2
  3.4 0.9 %copy-done.2 = s32[256,128]{1,0:T(8,128)S(1)} copy-done((s32[256,128]{1,0:T(8,128)S(1)}, s32[256,128]{1,0:T(8,128)}, u32[]{:S(2)}) %copy-start.2) | copy-done | bytes 131096
  4.3 0.0 copy-start.3
  4.3 0.9 %copy-done.3 = bf16[192,256]{1,0:T(8,128)(2,1)S(1)} copy-done((bf16[192,256]{1,0:T(8,128)(2,1)S(1)}, bf16[192,256]{1,0:T(8,128)(2,1)}, u32[]{:S(2)}) %copy-start.3) | copy-done | bytes 98328
  5.2 0.0 copy-start.4
  5.2 0.8 copy-done.4
  6.0 0.0 copy-start.5
  6.0 0.7 copy-done.5
  6.7 75.6 %shard_map.111 = (bf16[192,256]{1,0:T(8,128)(2,1)S(1)}, bf16[192,128]{1,0:T(8,128)(2,1)S(1)}, f32[6,128]{1,0:T(8,128)S(1)}, f32[6,3,192]{2,1,0:T(4,128)S(1)}) custom-call(bf16[192,128]{1,0:T(8,128)(2,1)S(1)} %copy-done.4, bf16[192,256]{1,0:T(8,128)(2,1)S(1)} %copy-done.3, bf16[3,192,768]{2,1,0:T(8,128)(2,1)S(1)} %copy-done, f32[1,192]{1,0:T(1,128)S(1)} %bitcast.2, ...), custom_call_target="tpu_custom_call" | custom-call | tf_op jit(solution)/shard_map/pallas_call | solution.py:401
  82.3 0.6 copy.16
  83.0 0.6 copy.17
  83.6 0.6 copy.18
  84.2 0.6 copy.19
Async XLA Ops:
  0.6 0.7 copy-start.6
  0.6 0.7 copy-start.7
  1.3 1.2 %copy-start = (bf16[3,192,768]{2,1,0:T(8,128)(2,1)S(1)}, bf16[3,192,768]{2,1,0:T(8,128)(2,1)}, u32[]{:S(2)}) copy-start(bf16[3,192,768]{2,1,0:T(8,128)(2,1)} %weight.1) | copy-start | bytes 2654212
  2.5 0.9 %copy-start.1 = (bf16[768,128]{1,0:T(8,128)(2,1)S(1)}, bf16[768,128]{1,0:T(8,128)(2,1)}, u32[]{:S(2)}) copy-start(bf16[768,128]{1,0:T(8,128)(2,1)} %head.1) | copy-start | bytes 589828
  3.4 0.9 %copy-start.2 = (s32[256,128]{1,0:T(8,128)S(1)}, s32[256,128]{1,0:T(8,128)}, u32[]{:S(2)}) copy-start(s32[256,128]{1,0:T(8,128)} %counts.1) | copy-start | bytes 393220
  4.3 0.9 %copy-start.3 = (bf16[192,256]{1,0:T(8,128)(2,1)S(1)}, bf16[192,256]{1,0:T(8,128)(2,1)}, u32[]{:S(2)}) copy-start(bf16[192,256]{1,0:T(8,128)(2,1)} %skip.1) | copy-start | bytes 294916
  5.2 0.8 copy-start.4
  6.0 0.7 copy-start.5

commit v2 on v1

v2 whole, which is shorter than its diff:
```python
import functools
import math

import jax
import jax.numpy as jnp
from jax import lax
from jax.experimental import pallas as pl
from jax.experimental.pallas import tpu as pltpu
from jax.sharding import PartitionSpec as P

root_two_pi = 0.7978845608028654
cubic_coef = 0.044715
multi_weight = 5.0
pseudo_count = 0.5

CORES, XS, YS, HIS, MPS = 2, 4, 8, 2, 4
ROW = XS * CORES
FAR = YS * HIS
SEQ = FAR * ROW

F32 = jnp.float32
BF16 = jnp.bfloat16
VMEM_BYTES = 63 * 1024 * 1024
MESH = pl.DeviceIdType.MESH


def gelu_parts(v):
    tangent = jnp.tanh(root_two_pi * (v + cubic_coef * v * v * v))
    value = 0.5 * v * (1.0 + tangent)
    slope = 0.5 * (1.0 + tangent) + 0.5 * v * (1.0 - tangent * tangent) * root_two_pi * (
        1.0 + 3.0 * cubic_coef * v * v
    )
    return value, slope


def dot(left, right, dims):
    return lax.dot_general(left, right, (dims, ((), ())), preferred_element_type=F32)


NN = ((1,), (0,))
NT = ((1,), (1,))
TN = ((0,), (0,))


def iota(shape, axis):
    return lax.broadcasted_iota(jnp.int32, shape, axis)


def one_hot(mask):
    return jnp.where(mask, 1.0, 0.0).astype(BF16)


def body(
    coarse_in, skip_in, weight_in, conv_bias_in, head_in, head_bias_in, counts_in, seg_mask_in,
    out_skip, out_coarse, out_head, out_conv,
    coarse, skip, weight, conv_bias, head, head_bias, counts, seg_mask,
    summed_all, edge_own, edge_all, hidden_all, head_own, track_all, seg_all,
    slope_ref, grad_hidden_ref, gb_ref, gedge, shifted,
    pick, summed_pick, hidden_pick, turned,
    back_send, back_recv,
    top_own, top_core_send, top_core_recv, top_x_send, top_x_recv, top_far_send, top_far_recv,
    own_half, core_send, core_recv, x_send, x_recv, far_own, far_send, far_recv,
    res_skip, res_coarse, res_head, res_conv,
    in_sems, out_sems, edge_sems, sum_sems, hid_sems, head_sems, seg_sems, track_sems,
    gedge_sems, back_sems, top_core_sems, top_x_sems, top_far_sems, core_sems, x_sems, far_sems,
):
    width, length = skip.shape
    half = length // 2
    channels = head.shape[0]
    tracks = head.shape[1]
    unit = channels // SEQ
    group = channels // ROW
    cols = core_send.shape[1]
    conv_cols = 3 * width
    scale_back = 1.0 / math.sqrt(length * SEQ)

    s = lax.axis_index("seq")
    z = lax.axis_index("mp")
    core = lax.rem(s, CORES)
    x = lax.rem(s // CORES, XS)
    y = lax.rem(s // ROW, YS)
    hi = s // (ROW * YS)
    mine = lax.rem(s, ROW)

    mp_peer = [lax.rem(z + d, MPS) for d in range(MPS)]
    row_peer = [s - mine + lax.rem(mine + d, ROW) for d in range(ROW)]
    core_peer = s + 1 - 2 * core
    x_peer = [s + CORES * (lax.rem(x + d, XS) - x) for d in range(XS)]
    far_peer = [
        s + ROW * (lax.rem(y + p // HIS, YS) - y) + ROW * YS * (lax.rem(hi + p % HIS, HIS) - hi)
        for p in range(FAR)
    ]
    right = lax.rem(s + 1, SEQ)
    left = lax.rem(s + SEQ - 1, SEQ)

    def send(src, dst, sems, slot, device):
        copy = pltpu.make_async_remote_copy(
            src_ref=src,
            dst_ref=dst,
            send_sem=sems.at[0, slot],
            recv_sem=sems.at[1, slot],
            device_id=device,
            device_id_type=MESH,
        )
        copy.start()
        return copy

    def store(src, dst, slot):
        copy = pltpu.make_async_copy(src, dst, out_sems.at[slot])
        copy.start()
        return copy

    def wait(copies):
        for copy in copies:
            copy.wait()

    barrier = pltpu.get_barrier_semaphore()
    greeted = [{"mp": p} for p in mp_peer[1:]]
    greeted += [{"seq": p, "mp": q} for p in (left, right) for q in mp_peer]
    greeted += [{"seq": p} for p in row_peer[1:] + far_peer[1:]]
    for device in greeted:
        pl.semaphore_signal(barrier, inc=1, device_id=device, device_id_type=MESH)

    loads = []
    for slot, (src, dst) in enumerate(
        (
            (coarse_in, coarse), (skip_in, skip), (weight_in, weight), (conv_bias_in, conv_bias),
            (head_in, head), (head_bias_in, head_bias), (counts_in, counts),
            (seg_mask_in, seg_mask),
        )
    ):
        copy = pltpu.make_async_copy(src, dst, in_sems.at[slot])
        copy.start()
        loads.append(copy)

    spread = one_hot(iota((half, length), 1) // 2 == iota((half, length), 0))
    edge_own[...] = jnp.zeros(edge_own.shape, BF16)
    wait(loads[:2])
    doubled = dot(coarse[...], spread, NN)
    summed = (doubled + skip[...].astype(F32)).astype(BF16)
    summed_all[z] = summed
    ends = one_hot(
        ((iota((16, length), 0) == 0) & (iota((16, length), 1) == 0))
        | ((iota((16, length), 0) == 1) & (iota((16, length), 1) == length - 1))
    )
    edge_own[:, 0:width] = dot(ends, summed, NT).astype(BF16)

    pl.semaphore_wait(barrier, len(greeted))

    edge_copies = []
    for side, neighbour in ((0, right), (1, left)):
        for d in range(MPS):
            edge_copies.append(
                send(
                    edge_own, edge_all.at[side, z], edge_sems, side * MPS + d,
                    {"seq": neighbour, "mp": mp_peer[d]},
                )
            )
    sum_copies = [
        send(summed_all.at[z], summed_all.at[z], sum_sems, d - 1, {"mp": mp_peer[d]})
        for d in range(1, MPS)
    ]

    row = iota((group, channels), 0)
    lane = iota((group, channels), 1)
    step = HIS * unit
    y_step = jnp.zeros_like(row)
    for j in range(1, YS):
        y_step = y_step + jnp.where(row >= step * j, 1, 0)
    rest = row - step * y_step
    hi_step = jnp.where(rest >= unit, 1, 0)
    rest = rest - unit * hi_step
    y_at = y + y_step
    y_at = jnp.where(y_at >= YS, y_at - YS, y_at)
    hi_at = jnp.where(hi_step == 1, 1 - hi, hi)
    base = ((hi_at * YS + y_at) * ROW) * unit + rest
    for c in range(CORES):
        core_at = core if c == 0 else 1 - core
        for d in range(XS):
            x_at = lax.rem(x + d, XS)
            place = (c * XS + d) * group
            pick[place : place + group, :] = one_hot(
                lane == base + (x_at * CORES + core_at) * unit
            )

    wait(loads[2:])
    for k in range(3):
        turned[k] = weight[k].T
    bias = conv_bias[...]
    part0 = bias.astype(BF16).astype(F32)
    part1 = (bias - part0).astype(BF16).astype(F32)
    part2 = bias - part0 - part1
    at = iota((16, width), 0)
    bias_rows = jnp.where(at == 0, part0, jnp.where(at == 1, part1, jnp.where(at == 2, part2, 0.0)))
    head_own[z] = head[pl.ds(pl.multiple_of(z * width, width), width), :]
    observed = counts[...].astype(F32)
    seg_all[mine] = jnp.zeros(seg_all.shape[1:], F32)
    seg_all[mine, 1:2, :] = jnp.sum(observed, axis=0, keepdims=True)
    far_own[...] = jnp.zeros(far_own.shape, F32)
    top_far_send[...] = jnp.zeros(top_far_send.shape, BF16)
    own_half[:, conv_cols:] = jnp.zeros((channels // 2, cols - conv_cols), F32)
    core_send[:, conv_cols:] = jnp.zeros((channels // 2, cols - conv_cols), BF16)

    wait(edge_copies)
    span = edge_all.shape[3]
    low_rows = jnp.zeros((16, channels), F32)
    high_rows = jnp.zeros((16, channels), F32)
    for k in range(MPS):
        placed = one_hot(
            (iota((span, channels), 1) == iota((span, channels), 0) + k * width)
            & (iota((span, channels), 0) < width)
        )
        low_rows = low_rows + dot(edge_all[0, k], placed, NN)
        high_rows = high_rows + dot(edge_all[1, k], placed, NN)
    keep_low = jnp.where(s == 0, 0.0, 1.0)
    keep_high = jnp.where(s == SEQ - 1, 0.0, 1.0)
    low_rows = (low_rows * keep_low).astype(BF16)
    high_rows = (high_rows * keep_high).astype(BF16)
    before = dot(bias_rows.astype(BF16), jnp.ones((16, length), BF16), TN)
    lanes = iota((width, length), 1)
    before = before + jnp.where(lanes == 0, dot(weight[0], low_rows, NT)[:, 1:2], 0.0)
    before = before + jnp.where(
        lanes == length - 1, dot(weight[2], high_rows, NT)[:, 0:1], 0.0
    )

    wait(sum_copies)
    summed_full = summed_all[...].reshape(channels, length)
    before = before + dot(weight[1], summed_full, NN)
    from_low = dot(weight[0], summed_full, NN)
    from_high = dot(weight[2], summed_full, NN)
    before = before + jnp.where(lanes == 0, 0.0, pltpu.roll(from_low, 1, 1))
    before = before + jnp.where(lanes == length - 1, 0.0, pltpu.roll(from_high, length - 1, 1))
    value, slope = gelu_parts(before)
    hidden_all[z] = (summed_all[z].astype(F32) + value).astype(BF16)
    hidden_copies = [
        send(hidden_all.at[z], hidden_all.at[z], hid_sems, d - 1, {"mp": mp_peer[d]})
        for d in range(1, MPS)
    ]
    slope_ref[...] = slope
    lanes_group = iota((group, length), 1)
    for k in range(ROW):
        at = slice(k * group, (k + 1) * group)
        picked = dot(pick[at, :], summed_full, NN)
        low_col = dot(pick[at, :], low_rows, NT)[:, 1:2]
        high_col = dot(pick[at, :], high_rows, NT)[:, 0:1]
        summed_pick[0, at, :] = jnp.where(
            lanes_group == 0, low_col, pltpu.roll(picked, 1, 1)
        ).astype(BF16)
        summed_pick[1, at, :] = picked.astype(BF16)
        summed_pick[2, at, :] = jnp.where(
            lanes_group == length - 1, high_col, pltpu.roll(picked, length - 1, 1)
        ).astype(BF16)

    wait(hidden_copies)
    hidden_full = hidden_all[...].reshape(channels, length)
    logits = dot(hidden_full, head[...], TN) + head_bias[...]
    small = jnp.exp(-jnp.abs(logits))
    predicted = jnp.maximum(logits, 0.0) + jnp.log1p(small) + pseudo_count
    seg_all[mine, 0:1, :] = jnp.sum(predicted, axis=0, keepdims=True)
    seg_copies = [
        send(seg_all.at[mine], seg_all.at[mine], seg_sems, d - 1, {"seq": row_peer[d]})
        for d in range(1, ROW)
    ]
    head_copies = [
        send(
            head.at[pl.ds(pl.multiple_of(mp_peer[d] * width, width), width), :],
            head_own.at[z],
            head_sems,
            d - 1,
            {"mp": mp_peer[d]},
        )
        for d in range(1, MPS)
    ]
    hidden_pick[...] = dot(pick[...], hidden_full, NN).astype(BF16)
    sigmoid = jnp.where(logits >= 0.0, 1.0, small) / (1.0 + small)
    ratio = multi_weight * observed / predicted
    mask_row = seg_mask[pl.ds(s // ROW, 1), :].astype(F32)
    wait(seg_copies)
    totals = seg_all[0]
    for k in range(1, ROW):
        totals = totals + seg_all[k]
    share = 1.0 + (multi_weight - 1.0) * totals[1:2, :] / totals[0:1, :]
    grad_logits = (mask_row * (share - ratio) * sigmoid).astype(BF16)
    track_all[z] = grad_logits
    track_copies = [
        send(track_all.at[z], track_all.at[z], track_sems, d - 1, {"mp": mp_peer[d]})
        for d in range(1, MPS)
    ]
    top_core_send[...] = dot(hidden_pick[channels // 2 :, :], grad_logits, NN).astype(BF16)
    top_core_copy = send(top_core_send, top_core_recv, top_core_sems, 0, {"seq": core_peer})
    top_own[...] = dot(hidden_pick[: channels // 2, :], grad_logits, NN)
    wait([top_core_copy])
    for d in range(1, XS):
        at = slice(d * group, (d + 1) * group)
        top_x_send[d - 1] = (top_own[at, :] + top_core_recv[at, :].astype(F32)).astype(BF16)
    top_x_copies = [
        send(top_x_send.at[d - 1], top_x_recv.at[d - 1], top_x_sems, d - 1, {"seq": x_peer[d]})
        for d in range(1, XS)
    ]

    wait(head_copies)
    wait(track_copies)
    grad_hidden = dot(head_own[0], track_all[0], NT)
    for k in range(1, MPS):
        grad_hidden = grad_hidden + dot(head_own[k], track_all[k], NT)
    gb = (grad_hidden * slope_ref[...]).astype(BF16)
    gb_ref[...] = gb
    gedge_copies = [
        send(gb_ref.at[:, pl.ds(half, half)], gedge.at[0], gedge_sems, 0, {"seq": right}),
        send(gb_ref.at[:, pl.ds(0, half)], gedge.at[1], gedge_sems, 1, {"seq": left}),
    ]

    for k in range(ROW // 2, ROW):
        at = slice((k - ROW // 2) * group, (k - ROW // 2 + 1) * group)
        for tap in range(3):
            part = dot(summed_pick[tap, k * group : (k + 1) * group, :], gb, NT)
            core_send[at, tap * width : (tap + 1) * width] = part.astype(BF16)
    core_copy = send(core_send, core_recv, core_sems, 0, {"seq": core_peer})
    grad_hidden_ref[...] = grad_hidden
    for k in range(ROW // 2):
        at = slice(k * group, (k + 1) * group)
        for tap in range(3):
            part = dot(summed_pick[tap, at, :], gb, NT)
            own_half[at, tap * width : (tap + 1) * width] = part
    wait([core_copy])
    for d in range(1, XS):
        at = slice(d * group, (d + 1) * group)
        x_send[d - 1] = (own_half[at, :] + core_recv[at, :].astype(F32)).astype(BF16)
    x_copies = [
        send(x_send.at[d - 1], x_recv.at[d - 1], x_sems, d - 1, {"seq": x_peer[d]})
        for d in range(1, XS)
    ]
    own_half[0:group, :] += core_recv[0:group, :].astype(F32)

    wait(top_x_copies)
    total = top_own[0:group, :] + top_core_recv[0:group, :].astype(F32)
    for d in range(1, XS):
        total = total + top_x_recv[d - 1].astype(F32)
    top_own[0:group, :] = total
    for p in range(1, FAR):
        top_far_send[p - 1, 0:unit, :] = top_own[p * unit : (p + 1) * unit, :].astype(BF16)
    top_far_copies = [
        send(
            top_far_send.at[p - 1], top_far_recv.at[p - 1], top_far_sems, p - 1,
            {"seq": far_peer[p]},
        )
        for p in range(1, FAR)
    ]

    gb_wide = gb_ref[...].astype(F32)
    to_left = pltpu.roll(gb_wide, length - 1, 1)
    to_right = pltpu.roll(gb_wide, 1, 1)
    shifted[width : 2 * width, :] = gb_ref[...]
    wait(gedge_copies)
    low_col = gedge[0].astype(F32)[:, half - 1 : half] * keep_low
    high_col = gedge[1].astype(F32)[:, 0:1] * keep_high
    shifted[0:width, :] = jnp.where(lanes == length - 1, high_col, to_left).astype(BF16)
    shifted[2 * width :, :] = jnp.where(lanes == 0, low_col, to_right).astype(BF16)
    back_copies = []
    for d in (1, 2, 3, 0):
        at = pl.ds(pl.multiple_of(mp_peer[d] * width, width), width)
        total = jnp.zeros((width, length), F32)
        for k in range(3):
            total = total + dot(turned[k, at, :], shifted[k * width : (k + 1) * width, :], NN)
        if d == 0:
            grad_hidden_ref[...] += total
        else:
            back_send[d - 1] = total.astype(BF16)
            back_copies.append(
                send(back_send.at[d - 1], back_recv.at[d - 1], back_sems, d - 1, {"mp": mp_peer[d]})
            )

    wait(x_copies)
    total = own_half[0:group, :]
    for d in range(1, XS):
        total = total + x_recv[d - 1].astype(F32)
    own_half[0:group, :] = total
    tiles = cols // 128
    far_copies = []
    for p in list(range(1, FAR)) + [0]:
        for j in range(tiles):
            far_own[p, j * unit : (j + 1) * unit, :] = own_half[
                p * unit : (p + 1) * unit, j * 128 : (j + 1) * 128
            ]
        if p > 0:
            far_send[p - 1] = far_own[p].astype(BF16)
            far_copies.append(
                send(far_send.at[p - 1], far_recv.at[p - 1], far_sems, p - 1, {"seq": far_peer[p]})
            )

    wait(back_copies)
    total = grad_hidden_ref[...]
    for d in range(1, MPS):
        total = total + back_recv[d - 1].astype(F32)
    res_skip[...] = total.astype(BF16)
    stores = [store(res_skip, out_skip, 0)]
    high = total.astype(BF16)
    rest = total - high.astype(F32)
    mid = rest.astype(BF16)
    low = (rest - mid.astype(F32)).astype(BF16)
    pairs = dot(high, spread, NT) + dot(mid, spread, NT) + dot(low, spread, NT)
    res_coarse[...] = pairs.astype(BF16)
    stores.append(store(res_coarse, out_coarse, 1))

    wait(top_far_copies)
    total = top_own[0:16, :]
    for p in range(1, FAR):
        total = total + top_far_recv[p - 1].astype(F32)
    res_head[...] = total[0:unit, :] * scale_back
    stores.append(store(res_head, out_head, 2))

    wait(far_copies)
    total = far_own[0]
    for p in range(1, FAR):
        total = total + far_recv[p - 1].astype(F32)
    total = total * scale_back
    final = jnp.concatenate([total[j * unit : (j + 1) * unit, :] for j in range(tiles)], axis=1)
    for k in range(3):
        res_conv[:, k, :] = final[:, k * width : (k + 1) * width]
    stores.append(store(res_conv, out_conv, 3))
    wait(stores)


def write_out(*refs):
    count = len(refs) // 2
    sems = refs[-1]
    copies = [
        pltpu.make_async_copy(refs[k], refs[count + k], sems.at[k]) for k in range(count)
    ]
    for copy in copies:
        copy.start()
    for copy in copies:
        copy.wait()


def shards(coarse, skip, conv_weight, conv_bias, head_weight, head_bias, counts, seg_mask):
    width, length = skip.shape
    channels, tracks = head_weight.shape
    half = length // 2
    group = channels // ROW
    cols = -(-3 * width // 128) * 128
    unit = channels // SEQ
    wide = -(-width // 128) * 128
    packed = -(-unit * (cols // 128) // 16) * 16

    args = (
        coarse, skip, conv_weight, conv_bias.reshape(1, -1), head_weight,
        head_bias.reshape(1, -1), counts, seg_mask,
    )

    shapes = (
        jax.ShapeDtypeStruct((width, length), BF16),
        jax.ShapeDtypeStruct((width, half), BF16),
        jax.ShapeDtypeStruct((unit, tracks), F32),
        jax.ShapeDtypeStruct((unit, 3, width), F32),
    )

    def sems(count):
        return pltpu.SemaphoreType.DMA((2, count))

    scratch = [pltpu.VMEM(a.shape, a.dtype) for a in args]
    scratch += [
        pltpu.VMEM((MPS, width, length), BF16),
        pltpu.VMEM((16, wide), BF16),
        pltpu.VMEM((2, MPS, 16, wide), BF16),
        pltpu.VMEM((MPS, width, length), BF16),
        pltpu.VMEM((MPS, width, tracks), BF16),
        pltpu.VMEM((MPS, length, tracks), BF16),
        pltpu.VMEM((ROW, 8, tracks), F32),
        pltpu.VMEM((width, length), F32),
        pltpu.VMEM((width, length), F32),
        pltpu.VMEM((width, length), BF16),
        pltpu.VMEM((2, width, half), BF16),
        pltpu.VMEM((3 * width, length), BF16),
        pltpu.VMEM((channels, channels), BF16),
        pltpu.VMEM((3, channels, length), BF16),
        pltpu.VMEM((channels, length), BF16),
        pltpu.VMEM((3, channels, width), BF16),
        pltpu.VMEM((MPS - 1, width, length), BF16),
        pltpu.VMEM((MPS - 1, width, length), BF16),
        pltpu.VMEM((channels // 2, tracks), F32),
        pltpu.VMEM((channels // 2, tracks), BF16),
        pltpu.VMEM((channels // 2, tracks), BF16),
        pltpu.VMEM((XS - 1, group, tracks), BF16),
        pltpu.VMEM((XS - 1, group, tracks), BF16),
        pltpu.VMEM((FAR - 1, 16, tracks), BF16),
        pltpu.VMEM((FAR - 1, 16, tracks), BF16),
        pltpu.VMEM((channels // 2, cols), F32),
        pltpu.VMEM((channels // 2, cols), BF16),
        pltpu.VMEM((channels // 2, cols), BF16),
        pltpu.VMEM((XS - 1, group, cols), BF16),
        pltpu.VMEM((XS - 1, group, cols), BF16),
        pltpu.VMEM((FAR, packed, 128), F32),
        pltpu.VMEM((FAR - 1, packed, 128), BF16),
        pltpu.VMEM((FAR - 1, packed, 128), BF16),
        *(pltpu.VMEM(a.shape, a.dtype) for a in shapes),
        pltpu.SemaphoreType.DMA((len(args),)),
        pltpu.SemaphoreType.DMA((len(shapes),)),
        sems(2 * MPS), sems(MPS - 1), sems(MPS - 1), sems(MPS - 1), sems(ROW - 1),
        sems(MPS - 1), sems(2), sems(MPS - 1), sems(1), sems(XS - 1), sems(FAR - 1),
        sems(1), sems(XS - 1), sems(FAR - 1),
    ]
    hbm = pl.BlockSpec(memory_space=pltpu.HBM)
    results = pl.pallas_call(
        body,
        out_shape=shapes,
        in_specs=[hbm] * len(args),
        out_specs=(hbm,) * len(shapes),
        scratch_shapes=scratch,
        compiler_params=pltpu.CompilerParams(
            collective_id=0, has_side_effects=True, vmem_limit_bytes=VMEM_BYTES
        ),
    )(*args)
    return pl.pallas_call(
        write_out,
        out_shape=shapes,
        in_specs=[hbm] * len(shapes),
        out_specs=(hbm,) * len(shapes),
        scratch_shapes=[pltpu.SemaphoreType.DMA((len(shapes),))],
        compiler_params=pltpu.CompilerParams(vmem_limit_bytes=VMEM_BYTES),
    )(*results)


def solution(mesh):
    in_specs = (
        P("mp", "seq"),
        P("mp", "seq"),
        P(None, "mp", None),
        P("mp"),
        P(None, "mp"),
        P("mp"),
        P("seq", "mp"),
        P(None, "mp"),
    )
    out_specs = (P("mp", "seq"), P("mp", "seq"), P("seq", "mp"), P("seq", None, "mp"))
    return jax.shard_map(shards, mesh=mesh, in_specs=in_specs, out_specs=out_specs, check_vma=False)
```

time: 85.1 us -> 77.5 us (0.911)
  the two profiles are of different devices: /device:TPU:16 before, /device:TPU:65 now
where the time goes in v2:
time: 77.5 us; the launch traced here: 77.3 us
  Pallas kernels  76.7 us (99%)
    pallas_call x1, Pallas kernels, shards(): pl.pallas_call(body, out_shape=shapes, in_specs=[hbm] * len(args), out_sp...  70.2 us
    pallas_call x1, Pallas kernels, shards(): pl.pallas_call(write_out, out_shape=shapes, in_specs=[hbm] * len(shapes),...  6.44 us

profile of v2, /device:TPU:65, one launch (start us, length us, event | category | flops | bytes accessed | tf_op | source)
XLA Modules:
  0.0 77.3 jit_solution(13258568604346215707)
XLA Ops:
  0.6 70.2 %shard_map.111 = (bf16[192,256]{1,0:T(8,128)(2,1)}, bf16[192,128]{1,0:T(8,128)(2,1)}, f32[6,128]{1,0:T(8,128)}, f32[6,3,192]{2,1,0:T(4,128)}) custom-call(bf16[192,128]{1,0:T(8,128)(2,1)} %coarse_in.1, bf16[192,256]{1,0:T(8,128)(2,1)} %skip_in.1, bf16[3,192,768]{2,1,0:T(8,128)(2,1)} %weight_in.1, f32[1,192]{1,0:T(1,128)} %bitcast.2, ...), custom_call_target="tpu_custom_call" | custom-call | tf_op jit(solution)/shard_map/pallas_call | solution.py:504
  70.9 6.4 %shard_map.112 = (bf16[192,256]{1,0:T(8,128)(2,1)}, bf16[192,128]{1,0:T(8,128)(2,1)}, f32[6,128]{1,0:T(8,128)}, f32[6,3,192]{2,1,0:T(4,128)}) custom-call(bf16[192,256]{1,0:T(8,128)(2,1)} %get-tuple-element.8.refs_0_, bf16[192,128]{1,0:T(8,128)(2,1)} %get-tuple-element.9.refs_1_, f32[6,128]{1,0:T(8,128)} %get-tuple-element.10.refs_2_, ...), custom_call_target="tpu_custom_call" | custom-call | tf_op jit(solution)/shard_map/pallas_call | solution.py:514

commit v3 on v2

v3 whole, which is shorter than its diff:
```python
import functools
import math

import jax
import jax.numpy as jnp
from jax import lax
from jax.experimental import pallas as pl
from jax.experimental.pallas import tpu as pltpu
from jax.sharding import PartitionSpec as P

root_two_pi = 0.7978845608028654
cubic_coef = 0.044715
multi_weight = 5.0
pseudo_count = 0.5

CORES, XS, YS, HIS, MPS = 2, 4, 8, 2, 4
ROW = XS * CORES
FAR = YS * HIS
SEQ = FAR * ROW

F32 = jnp.float32
BF16 = jnp.bfloat16
VMEM_BYTES = 63 * 1024 * 1024
MESH = pl.DeviceIdType.MESH


def gelu_parts(v):
    tangent = jnp.tanh(root_two_pi * (v + cubic_coef * v * v * v))
    value = 0.5 * v * (1.0 + tangent)
    slope = 0.5 * (1.0 + tangent) + 0.5 * v * (1.0 - tangent * tangent) * root_two_pi * (
        1.0 + 3.0 * cubic_coef * v * v
    )
    return value, slope


def dot(left, right, dims):
    return lax.dot_general(left, right, (dims, ((), ())), preferred_element_type=F32)


NN = ((1,), (0,))
NT = ((1,), (1,))
TN = ((0,), (0,))


def iota(shape, axis):
    return lax.broadcasted_iota(jnp.int32, shape, axis)


def one_hot(mask):
    return jnp.where(mask, 1.0, 0.0).astype(BF16)


def body(
    coarse_in, skip_in, weight_in, conv_bias_in, head_in, head_bias_in, counts_in, seg_mask_in,
    out_skip, out_coarse, out_head, out_conv,
    coarse, skip, weight, conv_bias, head_bias, counts, seg_mask,
    summed_all, edge_own, edge_all, mid_all, hidden_all, head_wide, counts_all, count_all,
    small_all, seg_all, slope_ref, grad_hidden_ref, gb_ref, gedge, shifted,
    pick, summed_pick, hidden_pick, turned,
    back_send, back_recv,
    top_own, top_core_send, top_core_recv, top_x_send, top_x_recv, top_far_send, top_far_recv,
    a_own, a_core_send, a_core_recv, a_x_send, a_x_recv, a_far_own, a_far_send, a_far_recv,
    b_own, b_core_send, b_core_recv, b_x_send, b_x_recv, b_far_own, b_far_send, b_far_recv,
    res_skip, res_coarse, res_head, res_conv,
    in_sems, out_sems, edge_sems, mid_sems, sum_sems, hid_sems, head_sems, spread_sems,
    counts_sems, count_sems, small_sems, seg_sems,
    gedge_sems, back_sems, top_core_sems, top_x_sems, top_far_sems,
    a_core_sems, a_x_sems, a_far_sems, b_core_sems, b_x_sems, b_far_sems,
):
    width, length = skip.shape
    half = length // 2
    channels = head_in.shape[0]
    tracks = head_in.shape[1]
    unit = channels // SEQ
    group = channels // ROW
    scale_back = 1.0 / math.sqrt(length * SEQ)

    s = lax.axis_index("seq")
    z = lax.axis_index("mp")
    core = lax.rem(s, CORES)
    x = lax.rem(s // CORES, XS)
    y = lax.rem(s // ROW, YS)
    hi = s // (ROW * YS)
    mine = lax.rem(s, ROW)

    mp_peer = [lax.rem(z + d, MPS) for d in range(MPS)]
    row_peer = [s - mine + lax.rem(mine + d, ROW) for d in range(ROW)]
    core_peer = s + 1 - 2 * core
    x_peer = [s + CORES * (lax.rem(x + d, XS) - x) for d in range(XS)]
    far_peer = [
        s + ROW * (lax.rem(y + p // HIS, YS) - y) + ROW * YS * (lax.rem(hi + p % HIS, HIS) - hi)
        for p in range(FAR)
    ]
    right = lax.rem(s + 1, SEQ)
    left = lax.rem(s + SEQ - 1, SEQ)

    def send(src, dst, sems, slot, device):
        copy = pltpu.make_async_remote_copy(
            src_ref=src,
            dst_ref=dst,
            send_sem=sems.at[0, slot],
            recv_sem=sems.at[1, slot],
            device_id=device,
            device_id_type=MESH,
        )
        copy.start()
        return copy

    def store(src, dst, slot):
        copy = pltpu.make_async_copy(src, dst, out_sems.at[slot])
        copy.start()
        return copy

    def wait(copies):
        for copy in copies:
            copy.wait()

    barrier = pltpu.get_barrier_semaphore()
    greeted = [{"mp": p} for p in mp_peer[1:]]
    greeted += [{"seq": p, "mp": q} for p in (left, right) for q in mp_peer]
    greeted += [{"seq": p} for p in row_peer[1:] + far_peer[1:]]
    for device in greeted:
        pl.semaphore_signal(barrier, inc=1, device_id=device, device_id_type=MESH)

    loads = []
    for slot, (src, dst) in enumerate(
        (
            (coarse_in, coarse), (skip_in, skip), (head_in, head_wide.at[:, pl.ds(0, tracks)]),
            (counts_in, counts), (weight_in, weight), (conv_bias_in, conv_bias),
            (head_bias_in, head_bias), (seg_mask_in, seg_mask),
        )
    ):
        copy = pltpu.make_async_copy(src, dst, in_sems.at[slot])
        copy.start()
        loads.append(copy)

    spread = one_hot(iota((half, length), 1) // 2 == iota((half, length), 0))
    edge_own[...] = jnp.zeros(edge_own.shape, BF16)
    wait(loads[:2])
    doubled = dot(coarse[...], spread, NN)
    summed = (doubled + skip[...].astype(F32)).astype(BF16)
    summed_all[z] = summed
    shape = (16, length)
    at_row, at_lane = iota(shape, 0), iota(shape, 1)
    ends = one_hot(
        ((at_row == 0) & (at_lane == 0))
        | ((at_row == 1) & (at_lane == length - 1))
        | ((at_row == 2) & (at_lane == half))
    )
    edge_own[:, 0:width] = dot(ends, summed, NT).astype(BF16)
    mid_all[z] = edge_own[...]
    pl.semaphore_wait(barrier, len(greeted))

    lower, upper = pl.ds(0, half), pl.ds(half, half)
    edge_copies = []
    for side, neighbour in ((0, right), (1, left)):
        for d in range(MPS):
            edge_copies.append(
                send(
                    edge_own, edge_all.at[side, z], edge_sems, side * MPS + d,
                    {"seq": neighbour, "mp": mp_peer[d]},
                )
            )
    mid_copies = [
        send(edge_own, mid_all.at[z], mid_sems, d - 1, {"mp": mp_peer[d]}) for d in range(1, MPS)
    ]

    def gather(ref, lanes, sems, first):
        return [
            send(
                ref.at[z, :, lanes], ref.at[z, :, lanes], sems, first + d - 1, {"mp": mp_peer[d]}
            )
            for d in range(1, MPS)
        ]

    sum_low = gather(summed_all, lower, sum_sems, 0)
    wait(loads[2:3])
    my_rows = pl.ds(pl.multiple_of(mine * group, group), group)
    head_copies = [
        send(
            head_wide.at[my_rows, pl.ds(0, tracks)],
            head_wide.at[my_rows, pl.ds((MPS - d) * tracks, tracks)],
            head_sems,
            d - 1,
            {"mp": mp_peer[d]},
        )
        for d in range(1, MPS)
    ]
    sum_high = gather(summed_all, upper, sum_sems, MPS - 1)
    wait(loads[3:])
    observed = counts[...].astype(F32)
    counts_all[0] = observed.astype(BF16)
    count_all[mine] = jnp.zeros(count_all.shape[1:], F32)
    count_all[mine, 0:1, :] = jnp.sum(observed, axis=0, keepdims=True)
    count_copies = [
        send(count_all.at[mine], count_all.at[mine], count_sems, d - 1, {"seq": row_peer[d]})
        for d in range(1, ROW)
    ]

    row = iota((group, channels), 0)
    lane = iota((group, channels), 1)
    step = HIS * unit
    y_step = jnp.zeros_like(row)
    for j in range(1, YS):
        y_step = y_step + jnp.where(row >= step * j, 1, 0)
    rest = row - step * y_step
    hi_step = jnp.where(rest >= unit, 1, 0)
    rest = rest - unit * hi_step
    y_at = y + y_step
    y_at = jnp.where(y_at >= YS, y_at - YS, y_at)
    hi_at = jnp.where(hi_step == 1, 1 - hi, hi)
    base = ((hi_at * YS + y_at) * ROW) * unit + rest
    for c in range(CORES):
        core_at = core if c == 0 else 1 - core
        for d in range(XS):
            x_at = lax.rem(x + d, XS)
            place = (c * XS + d) * group
            pick[place : place + group, :] = one_hot(
                lane == base + (x_at * CORES + core_at) * unit
            )

    for k in range(3):
        turned[k] = weight[k].T
    bias = conv_bias[...]
    part0 = bias.astype(BF16).astype(F32)
    part1 = (bias - part0).astype(BF16).astype(F32)
    part2 = bias - part0 - part1
    at = iota((16, width), 0)
    bias_rows = jnp.where(at == 0, part0, jnp.where(at == 1, part1, jnp.where(at == 2, part2, 0.0)))
    bias_wide = dot(bias_rows.astype(BF16), jnp.ones((16, half), BF16), TN)
    a_far_own[...] = jnp.zeros(a_far_own.shape, F32)
    b_far_own[...] = jnp.zeros(b_far_own.shape, F32)
    top_far_send[...] = jnp.zeros(top_far_send.shape, BF16)
    b_cols = b_own.shape[1]
    b_own[:, width:] = jnp.zeros((channels // 2, b_cols - width), F32)
    b_core_send[:, width:] = jnp.zeros((channels // 2, b_cols - width), BF16)

    wait(edge_copies)
    wait(mid_copies)
    span = edge_all.shape[3]
    low_rows = jnp.zeros((16, channels), F32)
    high_rows = jnp.zeros((16, channels), F32)
    mid_rows = jnp.zeros((16, channels), F32)
    for k in range(MPS):
        placed = one_hot(
            (iota((span, channels), 1) == iota((span, channels), 0) + k * width)
            & (iota((span, channels), 0) < width)
        )
        low_rows = low_rows + dot(edge_all[0, k], placed, NN)
        high_rows = high_rows + dot(edge_all[1, k], placed, NN)
        mid_rows = mid_rows + dot(mid_all[k], placed, NN)
    keep_low = jnp.where(s == 0, 0.0, 1.0)
    keep_high = jnp.where(s == SEQ - 1, 0.0, 1.0)
    low_rows = (low_rows * keep_low).astype(BF16)
    high_rows = (high_rows * keep_high).astype(BF16)
    mid_rows = mid_rows.astype(BF16)
    low_col = dot(weight[0], low_rows, NT)[:, 1:2]
    mid_col = dot(weight[2], mid_rows, NT)[:, 2:3]
    high_col = dot(weight[2], high_rows, NT)[:, 0:1]
    lanes = iota((width, half), 1)

    def convolve(at, first_col, last_col):
        block = summed_all[:, :, at].reshape(channels, half)
        from_low = dot(weight[0], block, NN)
        from_high = dot(weight[2], block, NN)
        before = bias_wide + dot(weight[1], block, NN)
        before = before + jnp.where(lanes == 0, first_col, pltpu.roll(from_low, 1, 1))
        before = before + jnp.where(
            lanes == half - 1, last_col, pltpu.roll(from_high, half - 1, 1)
        )
        value, slope = gelu_parts(before)
        hidden_all[z, :, at] = (summed_all[z, :, at].astype(F32) + value).astype(BF16)
        slope_ref[:, at] = slope
        return from_low[:, half - 1 : half]

    wait(sum_low)
    next_col = convolve(slice(0, half), low_col, mid_col)
    hidden_low = gather(hidden_all, lower, hid_sems, 0)

    wait(head_copies)
    spread_copies = [
        send(
            head_wide.at[my_rows, pl.ds(tracks, (MPS - 1) * tracks)],
            head_wide.at[my_rows, pl.ds(tracks, (MPS - 1) * tracks)],
            spread_sems,
            d - 1,
            {"seq": row_peer[d]},
        )
        for d in range(1, ROW)
    ]

    wait(sum_high)
    convolve(slice(half, length), next_col, high_col)
    hidden_high = gather(hidden_all, upper, hid_sems, MPS - 1)

    wait(count_copies)
    counted = count_all[0]
    for k in range(1, ROW):
        counted = counted + count_all[k]
    small_all[0] = jnp.zeros(small_all.shape[1:], F32)
    small_all[0, 0:1, :] = head_bias[...]
    small_all[0, 1:2, :] = seg_mask[pl.ds(s // ROW, 1), :].astype(F32)
    small_all[0, 2:3, :] = counted[0:1, :]
    small_copies = [
        send(small_all.at[0], small_all.at[MPS - d], small_sems, d - 1, {"mp": mp_peer[d]})
        for d in range(1, MPS)
    ]

    summed_full = summed_all[...].reshape(channels, length)
    lanes_group = iota((group, length), 1)
    for k in range(ROW):
        at = slice(k * group, (k + 1) * group)
        picked = dot(pick[at, :], summed_full, NN)
        low_edge = dot(pick[at, :], low_rows, NT)[:, 1:2]
        high_edge = dot(pick[at, :], high_rows, NT)[:, 0:1]
        summed_pick[0, at, :] = jnp.where(
            lanes_group == 0, low_edge, pltpu.roll(picked, 1, 1)
        ).astype(BF16)
        summed_pick[1, at, :] = picked.astype(BF16)
        summed_pick[2, at, :] = jnp.where(
            lanes_group == length - 1, high_edge, pltpu.roll(picked, length - 1, 1)
        ).astype(BF16)

    wait(hidden_low)
    counts_copies = [
        send(counts_all.at[0], counts_all.at[MPS - d], counts_sems, d - 1, {"mp": mp_peer[d]})
        for d in range(1, MPS)
    ]
    wait(small_copies)
    wait(spread_copies)
    wait(hidden_high)
    hidden_full = hidden_all[...].reshape(channels, length)
    products = dot(hidden_full, head_wide[...], TN)
    sigmoids, inverses = [], []
    seg_all[mine] = jnp.zeros(seg_all.shape[1:], F32)
    for d in range(MPS):
        logits = products[:, d * tracks : (d + 1) * tracks] + small_all[d, 0:1, :]
        small = jnp.exp(-jnp.abs(logits))
        predicted = jnp.maximum(logits, 0.0) + jnp.log1p(small) + pseudo_count
        seg_all[mine, d : d + 1, :] = jnp.sum(predicted, axis=0, keepdims=True)
        sigmoids.append((logits, small))
        inverses.append(predicted)
    seg_copies = [
        send(seg_all.at[mine], seg_all.at[mine], seg_sems, d - 1, {"seq": row_peer[d]})
        for d in range(1, ROW)
    ]
    for d in range(MPS):
        logits, small = sigmoids[d]
        sigmoids[d] = small_all[d, 1:2, :] * jnp.where(logits >= 0.0, 1.0, small) / (1.0 + small)
        inverses[d] = multi_weight / inverses[d]
    hidden_pick[...] = dot(pick[...], hidden_full, NN).astype(BF16)
    wait(counts_copies)
    wait(seg_copies)
    totals = seg_all[0]
    for k in range(1, ROW):
        totals = totals + seg_all[k]
    blocks = []
    for d in range(MPS):
        share = 1.0 + (multi_weight - 1.0) * small_all[d, 2:3, :] / totals[d : d + 1, :]
        blocks.append(
            ((share - counts_all[d].astype(F32) * inverses[d]) * sigmoids[d]).astype(BF16)
        )
    grad_logits = blocks[0]
    own_rows = pl.ds(pl.multiple_of(z * width, width), width)
    grad_hidden = dot(head_wide[own_rows, :], jnp.concatenate(blocks, axis=1), NT)
    gb = (grad_hidden * slope_ref[...]).astype(BF16)
    gb_ref[...] = gb

    class Sums:
        def __init__(self, refs, sems):
            self.own, self.core_send, self.core_recv, self.x_send, self.x_recv = refs[:5]
            self.far_own, self.far_send, self.far_recv = refs[5:]
            self.core_sems, self.x_sems, self.far_sems = sems

        def to_core(self):
            self.core_copy = send(
                self.core_send, self.core_recv, self.core_sems, 0, {"seq": core_peer}
            )

        def to_x(self):
            self.core_copy.wait()
            self.x_copies = []
            for d in range(1, XS):
                at = slice(d * group, (d + 1) * group)
                self.x_send[d - 1] = (
                    self.own[at, :] + self.core_recv[at, :].astype(F32)
                ).astype(BF16)
                self.x_copies.append(
                    send(
                        self.x_send.at[d - 1], self.x_recv.at[d - 1], self.x_sems, d - 1,
                        {"seq": x_peer[d]},
                    )
                )
            self.own[0:group, :] += self.core_recv[0:group, :].astype(F32)

        def add_x(self):
            wait(self.x_copies)
            total = self.own[0:group, :]
            for d in range(1, XS):
                total = total + self.x_recv[d - 1].astype(F32)
            self.own[0:group, :] = total

        def to_far(self):
            self.add_x()
            self.far_copies = []
            for p in list(range(1, FAR)) + [0]:
                for j in range(self.own.shape[1] // 128):
                    self.far_own[p, j * unit : (j + 1) * unit, :] = self.own[
                        p * unit : (p + 1) * unit, j * 128 : (j + 1) * 128
                    ]
                if p > 0:
                    self.far_send[p - 1] = self.far_own[p].astype(BF16)
                    self.far_copies.append(
                        send(
                            self.far_send.at[p - 1], self.far_recv.at[p - 1], self.far_sems,
                            p - 1, {"seq": far_peer[p]},
                        )
                    )

        def end(self):
            wait(self.far_copies)
            total = self.far_own[0]
            for p in range(1, FAR):
                total = total + self.far_recv[p - 1].astype(F32)
            total = total * scale_back
            return jnp.concatenate(
                [total[j * unit : (j + 1) * unit, :] for j in range(self.own.shape[1] // 128)],
                axis=1,
            )

    sums_a = Sums(
        (a_own, a_core_send, a_core_recv, a_x_send, a_x_recv, a_far_own, a_far_send, a_far_recv),
        (a_core_sems, a_x_sems, a_far_sems),
    )
    sums_b = Sums(
        (b_own, b_core_send, b_core_recv, b_x_send, b_x_recv, b_far_own, b_far_send, b_far_recv),
        (b_core_sems, b_x_sems, b_far_sems),
    )

    def for_sibling(ref, taps):
        for k in range(ROW // 2, ROW):
            at = slice((k - ROW // 2) * group, (k - ROW // 2 + 1) * group)
            for place, tap in enumerate(taps):
                part = dot(summed_pick[tap, k * group : (k + 1) * group, :], gb, NT)
                ref[at, place * width : (place + 1) * width] = part.astype(BF16)

    def for_own(ref, taps):
        for k in range(ROW // 2):
            at = slice(k * group, (k + 1) * group)
            for place, tap in enumerate(taps):
                part = dot(summed_pick[tap, at, :], gb, NT)
                ref[at, place * width : (place + 1) * width] = part

    for_sibling(a_core_send, (0, 1))
    sums_a.to_core()
    gedge_copies = [
        send(gb_ref.at[:, upper], gedge.at[0], gedge_sems, 0, {"seq": right}),
        send(gb_ref.at[:, lower], gedge.at[1], gedge_sems, 1, {"seq": left}),
    ]
    for_sibling(b_core_send, (2,))
    sums_b.to_core()
    top_core_send[...] = dot(hidden_pick[channels // 2 :, :], grad_logits, NN).astype(BF16)
    top_core_copy = send(top_core_send, top_core_recv, top_core_sems, 0, {"seq": core_peer})
    for_own(a_own, (0, 1))
    sums_a.to_x()
    for_own(b_own, (2,))
    sums_b.to_x()
    grad_hidden_ref[...] = grad_hidden
    top_own[...] = dot(hidden_pick[: channels // 2, :], grad_logits, NN)
    wait([top_core_copy])
    for d in range(1, XS):
        at = slice(d * group, (d + 1) * group)
        top_x_send[d - 1] = (top_own[at, :] + top_core_recv[at, :].astype(F32)).astype(BF16)
    top_x_copies = [
        send(top_x_send.at[d - 1], top_x_recv.at[d - 1], top_x_sems, d - 1, {"seq": x_peer[d]})
        for d in range(1, XS)
    ]

    lanes = iota((width, length), 1)
    gb_wide = gb_ref[...].astype(F32)
    to_left = pltpu.roll(gb_wide, length - 1, 1)
    to_right = pltpu.roll(gb_wide, 1, 1)
    shifted[width : 2 * width, :] = gb_ref[...]

    def back_convolution():
        wait(gedge_copies)
        low_edge = gedge[0].astype(F32)[:, half - 1 : half] * keep_low
        high_edge = gedge[1].astype(F32)[:, 0:1] * keep_high
        shifted[0:width, :] = jnp.where(lanes == length - 1, high_edge, to_left).astype(BF16)
        shifted[2 * width :, :] = jnp.where(lanes == 0, low_edge, to_right).astype(BF16)
        copies = []
        for d in (1, 2, 3, 0):
            at = pl.ds(pl.multiple_of(mp_peer[d] * width, width), width)
            total = jnp.zeros((width, length), F32)
            for k in range(3):
                total = total + dot(turned[k, at, :], shifted[k * width : (k + 1) * width, :], NN)
            if d == 0:
                grad_hidden_ref[...] += total
            else:
                back_send[d - 1] = total.astype(BF16)
                copies.append(
                    send(
                        back_send.at[d - 1], back_recv.at[d - 1], back_sems, d - 1,
                        {"mp": mp_peer[d]},
                    )
                )
        return copies

    back_copies = back_convolution()
    sums_a.to_far()
    sums_b.to_far()

    wait(top_x_copies)
    total = top_own[0:group, :] + top_core_recv[0:group, :].astype(F32)
    for d in range(1, XS):
        total = total + top_x_recv[d - 1].astype(F32)
    top_own[0:group, :] = total
    for p in range(1, FAR):
        top_far_send[p - 1, 0:unit, :] = top_own[p * unit : (p + 1) * unit, :].astype(BF16)
    top_far_copies = [
        send(
            top_far_send.at[p - 1], top_far_recv.at[p - 1], top_far_sems, p - 1,
            {"seq": far_peer[p]},
        )
        for p in range(1, FAR)
    ]

    wait(back_copies)
    total = grad_hidden_ref[...]
    for d in range(1, MPS):
        total = total + back_recv[d - 1].astype(F32)
    res_skip[...] = total.astype(BF16)
    stores = [store(res_skip, out_skip, 0)]
    high = total.astype(BF16)
    rest = total - high.astype(F32)
    mid = rest.astype(BF16)
    low = (rest - mid.astype(F32)).astype(BF16)
    pairs = dot(high, spread, NT) + dot(mid, spread, NT) + dot(low, spread, NT)
    res_coarse[...] = pairs.astype(BF16)
    stores.append(store(res_coarse, out_coarse, 1))

    final = sums_a.end()
    for k in range(2):
        res_conv[:, k, :] = final[:, k * width : (k + 1) * width]
    final = sums_b.end()
    res_conv[:, 2, :] = final[:, 0:width]
    stores.append(store(res_conv, out_conv, 3))

    wait(top_far_copies)
    total = top_own[0:16, :]
    for p in range(1, FAR):
        total = total + top_far_recv[p - 1].astype(F32)
    res_head[...] = total[0:unit, :] * scale_back
    stores.append(store(res_head, out_head, 2))
    wait(stores)


def write_out(*refs):
    count = len(refs) // 2
    for k in range(count):
        refs[count + k][...] = refs[k][...]


def shards(coarse, skip, conv_weight, conv_bias, head_weight, head_bias, counts, seg_mask):
    width, length = skip.shape
    channels, tracks = head_weight.shape
    half = length // 2
    group = channels // ROW
    unit = channels // SEQ
    wide = -(-width // 128) * 128

    args = (
        coarse, skip, conv_weight, conv_bias.reshape(1, -1), head_weight,
        head_bias.reshape(1, -1), counts, seg_mask,
    )

    shapes = (
        jax.ShapeDtypeStruct((width, length), BF16),
        jax.ShapeDtypeStruct((width, half), BF16),
        jax.ShapeDtypeStruct((unit, tracks), F32),
        jax.ShapeDtypeStruct((unit, 3, width), F32),
    )

    def sems(count):
        return pltpu.SemaphoreType.DMA((2, count))

    def sums(cols):
        cols = -(-cols // 128) * 128
        packed = -(-unit * (cols // 128) // 16) * 16
        return [
            pltpu.VMEM((channels // 2, cols), F32),
            pltpu.VMEM((channels // 2, cols), BF16),
            pltpu.VMEM((channels // 2, cols), BF16),
            pltpu.VMEM((XS - 1, group, cols), BF16),
            pltpu.VMEM((XS - 1, group, cols), BF16),
            pltpu.VMEM((FAR, packed, 128), F32),
            pltpu.VMEM((FAR - 1, packed, 128), BF16),
            pltpu.VMEM((FAR - 1, packed, 128), BF16),
        ]

    scratch = [pltpu.VMEM(a.shape, a.dtype) for k, a in enumerate(args) if k != 4]
    scratch += [
        pltpu.VMEM((MPS, width, length), BF16),
        pltpu.VMEM((16, wide), BF16),
        pltpu.VMEM((2, MPS, 16, wide), BF16),
        pltpu.VMEM((MPS, 16, wide), BF16),
        pltpu.VMEM((MPS, width, length), BF16),
        pltpu.VMEM((channels, MPS * tracks), BF16),
        pltpu.VMEM((MPS, length, tracks), BF16),
        pltpu.VMEM((ROW, 8, tracks), F32),
        pltpu.VMEM((MPS, 8, tracks), F32),
        pltpu.VMEM((ROW, 8, tracks), F32),
        pltpu.VMEM((width, length), F32),
        pltpu.VMEM((width, length), F32),
        pltpu.VMEM((width, length), BF16),
        pltpu.VMEM((2, width, half), BF16),
        pltpu.VMEM((3 * width, length), BF16),
        pltpu.VMEM((channels, channels), BF16),
        pltpu.VMEM((3, channels, length), BF16),
        pltpu.VMEM((channels, length), BF16),
        pltpu.VMEM((3, channels, width), BF16),
        pltpu.VMEM((MPS - 1, width, length), BF16),
        pltpu.VMEM((MPS - 1, width, length), BF16),
        pltpu.VMEM((channels // 2, tracks), F32),
        pltpu.VMEM((channels // 2, tracks), BF16),
        pltpu.VMEM((channels // 2, tracks), BF16),
        pltpu.VMEM((XS - 1, group, tracks), BF16),
        pltpu.VMEM((XS - 1, group, tracks), BF16),
        pltpu.VMEM((FAR - 1, 16, tracks), BF16),
        pltpu.VMEM((FAR - 1, 16, tracks), BF16),
        *sums(2 * width),
        *sums(width),
        *(pltpu.VMEM(a.shape, a.dtype) for a in shapes),
        pltpu.SemaphoreType.DMA((len(args),)),
        pltpu.SemaphoreType.DMA((len(shapes),)),
        sems(2 * MPS), sems(MPS - 1), sems(2 * MPS - 2), sems(2 * MPS - 2), sems(MPS - 1),
        sems(ROW - 1), sems(MPS - 1), sems(ROW - 1), sems(MPS - 1), sems(ROW - 1),
        sems(2), sems(MPS - 1), sems(1), sems(XS - 1), sems(FAR - 1),
        sems(1), sems(XS - 1), sems(FAR - 1), sems(1), sems(XS - 1), sems(FAR - 1),
    ]
    vmem = pl.BlockSpec(memory_space=pltpu.VMEM)
    hbm = pl.BlockSpec(memory_space=pltpu.HBM)
    results = pl.pallas_call(
        body,
        out_shape=shapes,
        in_specs=[hbm] * len(args),
        out_specs=(hbm,) * len(shapes),
        scratch_shapes=scratch,
        compiler_params=pltpu.CompilerParams(
            collective_id=0, has_side_effects=True, vmem_limit_bytes=VMEM_BYTES
        ),
    )(*args)
    return pl.pallas_call(
        write_out,
        out_shape=shapes,
        in_specs=[vmem] * len(shapes),
        out_specs=(vmem,) * len(shapes),
        compiler_params=pltpu.CompilerParams(vmem_limit_bytes=VMEM_BYTES),
    )(*results)


def solution(mesh):
    in_specs = (
        P("mp", "seq"),
        P("mp", "seq"),
        P(None, "mp", None),
        P("mp"),
        P(None, "mp"),
        P("mp"),
        P("seq", "mp"),
        P(None, "mp"),
    )
    out_specs = (P("mp", "seq"), P("mp", "seq"), P("seq", "mp"), P("seq", None, "mp"))
    return jax.shard_map(shards, mesh=mesh, in_specs=in_specs, out_specs=out_specs, check_vma=False)
```

time: 77.5 us -> 72.1 us (0.930)
  the two profiles are of different devices: /device:TPU:65 before, /device:TPU:1 now
where the time goes in v3:
time: 72.1 us; the launch traced here: 71.3 us
  Pallas kernels  70.6 us (98%)
    pallas_call x1, Pallas kernels, shards(): pl.pallas_call(body, out_shape=shapes, in_specs=[hbm] * len(args), out_sp...  69 us
    pallas_call x1, Pallas kernels, shards(): pl.pallas_call(write_out, out_shape=shapes, in_specs=[vmem] * len(shapes)...  1.6 us

profile of v3, /device:TPU:1, one launch (start us, length us, event | category | flops | bytes accessed | tf_op | source)
XLA Modules:
  0.0 71.3 jit_solution(11031592809316386524)
XLA Ops:
  0.6 69.0 %shard_map.111 = (bf16[192,256]{1,0:T(8,128)(2,1)}, bf16[192,128]{1,0:T(8,128)(2,1)}, f32[6,128]{1,0:T(8,128)}, f32[6,3,192]{2,1,0:T(4,128)}) custom-call(bf16[192,128]{1,0:T(8,128)(2,1)} %coarse_in.1, bf16[192,256]{1,0:T(8,128)(2,1)} %skip_in.1, bf16[3,192,768]{2,1,0:T(8,128)(2,1)} %weight_in.1, f32[1,192]{1,0:T(1,128)} %bitcast.2, ...), custom_call_target="tpu_custom_call" | custom-call | tf_op jit(solution)/shard_map/pallas_call | solution.py:643
  69.7 1.6 %shard_map.112 = (bf16[192,256]{1,0:T(8,128)(2,1)}, bf16[192,128]{1,0:T(8,128)(2,1)}, f32[6,128]{1,0:T(8,128)}, f32[6,3,192]{2,1,0:T(4,128)}) custom-call(bf16[192,256]{1,0:T(8,128)(2,1)} %get-tuple-element.8.refs_0_, bf16[192,128]{1,0:T(8,128)(2,1)} %get-tuple-element.9.refs_1_, f32[6,128]{1,0:T(8,128)} %get-tuple-element.10.refs_2_, ...), custom_call_target="tpu_custom_call" | custom-call | tf_op jit(solution)/shard_map/pallas_call | solution.py:653

commit v4 on v3

--- a/solution.py
+++ b/solution.py
@@ -55,16 +55,15 @@
     out_skip, out_coarse, out_head, out_conv,
     coarse, skip, weight, conv_bias, head_bias, counts, seg_mask,
     summed_all, edge_own, edge_all, mid_all, hidden_all, head_wide, counts_all, count_all,
-    small_all, seg_all, slope_ref, grad_hidden_ref, gb_ref, gedge, shifted,
+    small_all, seg_all, slope_ref, grad_hidden_ref, gb_ref, edge_send, edge_recv, shifted,
     pick, summed_pick, hidden_pick, turned,
     back_send, back_recv,
-    top_own, top_core_send, top_core_recv, top_x_send, top_x_recv, top_far_send, top_far_recv,
     a_own, a_core_send, a_core_recv, a_x_send, a_x_recv, a_far_own, a_far_send, a_far_recv,
     b_own, b_core_send, b_core_recv, b_x_send, b_x_recv, b_far_own, b_far_send, b_far_recv,
     res_skip, res_coarse, res_head, res_conv,
     in_sems, out_sems, edge_sems, mid_sems, sum_sems, hid_sems, head_sems, spread_sems,
     counts_sems, count_sems, small_sems, seg_sems,
-    gedge_sems, back_sems, top_core_sems, top_x_sems, top_far_sems,
+    gedge_sems, back_sems,
     a_core_sems, a_x_sems, a_far_sems, b_core_sems, b_x_sems, b_far_sems,
 ):
     width, length = skip.shape
@@ -135,20 +134,25 @@
         loads.append(copy)
 
     spread = one_hot(iota((half, length), 1) // 2 == iota((half, length), 0))
-    edge_own[...] = jnp.zeros(edge_own.shape, BF16)
     wait(loads[:2])
     doubled = dot(coarse[...], spread, NN)
     summed = (doubled + skip[...].astype(F32)).astype(BF16)
     summed_all[z] = summed
     shape = (16, length)
     at_row, at_lane = iota(shape, 0), iota(shape, 1)
-    ends = one_hot(
-        ((at_row == 0) & (at_lane == 0))
-        | ((at_row == 1) & (at_lane == length - 1))
-        | ((at_row == 2) & (at_lane == half))
-    )
-    edge_own[:, 0:width] = dot(ends, summed, NT).astype(BF16)
+    ends = [
+        one_hot(
+            ((at_row == k) & (at_lane == 0))
+            | ((at_row == k + 2) & (at_lane == length - 1))
+            | ((at_row == k + 4) & (at_lane == half))
+        )
+        for k in range(2)
+    ]
+    short = width - 128
+    upper_rows = jnp.concatenate([summed[128:, :], jnp.zeros((128 - short, length), BF16)], axis=0)
+    edge_own[...] = (dot(ends[0], summed[0:128, :], NT) + dot(ends[1], upper_rows, NT)).astype(BF16)
     mid_all[z] = edge_own[...]
+    edge_send[...] = jnp.zeros(edge_send.shape, F32)
     pl.semaphore_wait(barrier, len(greeted))
 
     lower, upper = pl.ds(0, half), pl.ds(half, half)
@@ -230,32 +234,36 @@
     bias_wide = dot(bias_rows.astype(BF16), jnp.ones((16, half), BF16), TN)
     a_far_own[...] = jnp.zeros(a_far_own.shape, F32)
     b_far_own[...] = jnp.zeros(b_far_own.shape, F32)
-    top_far_send[...] = jnp.zeros(top_far_send.shape, BF16)
     b_cols = b_own.shape[1]
-    b_own[:, width:] = jnp.zeros((channels // 2, b_cols - width), F32)
-    b_core_send[:, width:] = jnp.zeros((channels // 2, b_cols - width), BF16)
+    b_own[:, width : b_cols - tracks] = jnp.zeros((channels // 2, b_cols - tracks - width), F32)
+    b_core_send[:, width : b_cols - tracks] = jnp.zeros(
+        (channels // 2, b_cols - tracks - width), BF16
+    )
 
     wait(edge_copies)
     wait(mid_copies)
-    span = edge_all.shape[3]
-    low_rows = jnp.zeros((16, channels), F32)
-    high_rows = jnp.zeros((16, channels), F32)
-    mid_rows = jnp.zeros((16, channels), F32)
-    for k in range(MPS):
-        placed = one_hot(
-            (iota((span, channels), 1) == iota((span, channels), 0) + k * width)
-            & (iota((span, channels), 0) < width)
-        )
-        low_rows = low_rows + dot(edge_all[0, k], placed, NN)
-        high_rows = high_rows + dot(edge_all[1, k], placed, NN)
-        mid_rows = mid_rows + dot(mid_all[k], placed, NN)
+    at_row, at_lane = iota((128, channels), 0), iota((128, channels), 1)
+
+    def unpack(ref):
+        first = jnp.zeros((16, channels), F32)
+        second = jnp.zeros((16, channels), F32)
+        for k in range(MPS):
+            placed = one_hot(at_lane == at_row + k * width)
+            first = first + dot(ref[k], placed, NN)
+            placed = one_hot((at_lane == at_row + (k * width + 128)) & (at_row < short))
+            second = second + dot(ref[k], placed, NN)
+        return first + pltpu.roll(second, 15, 0)
+
+    low_rows = unpack(edge_all.at[0])
+    high_rows = unpack(edge_all.at[1])
+    mid_rows = unpack(mid_all)
     keep_low = jnp.where(s == 0, 0.0, 1.0)
     keep_high = jnp.where(s == SEQ - 1, 0.0, 1.0)
     low_rows = (low_rows * keep_low).astype(BF16)
     high_rows = (high_rows * keep_high).astype(BF16)
     mid_rows = mid_rows.astype(BF16)
-    low_col = dot(weight[0], low_rows, NT)[:, 1:2]
-    mid_col = dot(weight[2], mid_rows, NT)[:, 2:3]
+    low_col = dot(weight[0], low_rows, NT)[:, 2:3]
+    mid_col = dot(weight[2], mid_rows, NT)[:, 4:5]
     high_col = dot(weight[2], high_rows, NT)[:, 0:1]
     lanes = iota((width, half), 1)
 
@@ -311,7 +319,7 @@
     for k in range(ROW):
         at = slice(k * group, (k + 1) * group)
         picked = dot(pick[at, :], summed_full, NN)
-        low_edge = dot(pick[at, :], low_rows, NT)[:, 1:2]
+        low_edge = dot(pick[at, :], low_rows, NT)[:, 2:3]
         high_edge = dot(pick[at, :], high_rows, NT)[:, 0:1]
         summed_pick[0, at, :] = jnp.where(
             lanes_group == 0, low_edge, pltpu.roll(picked, 1, 1)
@@ -321,14 +329,16 @@
             lanes_group == length - 1, high_edge, pltpu.roll(picked, length - 1, 1)
         ).astype(BF16)
 
-    wait(hidden_low)
+    for copy in hidden_low + hidden_high:
+        copy.wait_send()
     counts_copies = [
         send(counts_all.at[0], counts_all.at[MPS - d], counts_sems, d - 1, {"mp": mp_peer[d]})
         for d in range(1, MPS)
     ]
     wait(small_copies)
     wait(spread_copies)
-    wait(hidden_high)
+    for copy in hidden_low + hidden_high:
+        copy.wait_recv()
     hidden_full = hidden_all[...].reshape(channels, length)
     products = dot(hidden_full, head_wide[...], TN)
     sigmoids, inverses = [], []
@@ -453,80 +463,66 @@
 
     for_sibling(a_core_send, (0, 1))
     sums_a.to_core()
-    gedge_copies = [
-        send(gb_ref.at[:, upper], gedge.at[0], gedge_sems, 0, {"seq": right}),
-        send(gb_ref.at[:, lower], gedge.at[1], gedge_sems, 1, {"seq": left}),
-    ]
+    gb_ends = dot(ends[0], gb, NT).astype(BF16)
+    for side, tap, at in ((0, 2, 2), (1, 0, 0)):
+        term = dot(gb_ends, weight[tap], NN)
+        for k in range(MPS):
+            edge_send[side, k, 0:1, :] = term[at : at + 1, k * width : k * width + 128]
+            edge_send[side, k, 1:2, 0:short] = term[at : at + 1, k * width + 128 : (k + 1) * width]
+    gedge_copies = []
+    for side, neighbour in ((0, right), (1, left)):
+        for d in range(MPS):
+            gedge_copies.append(
+                send(
+                    edge_send.at[side, mp_peer[d]], edge_recv.at[side, z], gedge_sems,
+                    side * MPS + d, {"seq": neighbour, "mp": mp_peer[d]},
+                )
+            )
     for_sibling(b_core_send, (2,))
+    b_core_send[:, b_cols - tracks :] = dot(
+        hidden_pick[channels // 2 :, :], grad_logits, NN
+    ).astype(BF16)
     sums_b.to_core()
-    top_core_send[...] = dot(hidden_pick[channels // 2 :, :], grad_logits, NN).astype(BF16)
-    top_core_copy = send(top_core_send, top_core_recv, top_core_sems, 0, {"seq": core_peer})
+    lanes = iota((width, length), 1)
+    gb_wide = gb.astype(F32)
+    shifted[0:width, :] = jnp.where(
+        lanes == length - 1, 0.0, pltpu.roll(gb_wide, length - 1, 1)
+    ).astype(BF16)
+    shifted[width : 2 * width, :] = gb
+    shifted[2 * width :, :] = jnp.where(lanes == 0, 0.0, pltpu.roll(gb_wide, 1, 1)).astype(BF16)
+
+    def back(owner):
+        at = pl.ds(pl.multiple_of(owner * width, width), width)
+        total = dot(turned[0, at, :], shifted[0:width, :], NN)
+        for k in range(1, 3):
+            total = total + dot(turned[k, at, :], shifted[k * width : (k + 1) * width, :], NN)
+        return total
+
+    back_copies = []
+    for d in range(1, MPS):
+        back_send[d - 1] = back(mp_peer[d]).astype(BF16)
+        back_copies.append(
+            send(back_send.at[d - 1], back_recv.at[d - 1], back_sems, d - 1, {"mp": mp_peer[d]})
+        )
     for_own(a_own, (0, 1))
     sums_a.to_x()
     for_own(b_own, (2,))
+    b_own[:, b_cols - tracks :] = dot(hidden_pick[: channels // 2, :], grad_logits, NN)
     sums_b.to_x()
-    grad_hidden_ref[...] = grad_hidden
-    top_own[...] = dot(hidden_pick[: channels // 2, :], grad_logits, NN)
-    wait([top_core_copy])
-    for d in range(1, XS):
-        at = slice(d * group, (d + 1) * group)
-        top_x_send[d - 1] = (top_own[at, :] + top_core_recv[at, :].astype(F32)).astype(BF16)
-    top_x_copies = [
-        send(top_x_send.at[d - 1], top_x_recv.at[d - 1], top_x_sems, d - 1, {"seq": x_peer[d]})
-        for d in range(1, XS)
-    ]
-
-    lanes = iota((width, length), 1)
-    gb_wide = gb_ref[...].astype(F32)
-    to_left = pltpu.roll(gb_wide, length - 1, 1)
-    to_right = pltpu.roll(gb_wide, 1, 1)
-    shifted[width : 2 * width, :] = gb_ref[...]
-
-    def back_convolution():
-        wait(gedge_copies)
-        low_edge = gedge[0].astype(F32)[:, half - 1 : half] * keep_low
-        high_edge = gedge[1].astype(F32)[:, 0:1] * keep_high
-        shifted[0:width, :] = jnp.where(lanes == length - 1, high_edge, to_left).astype(BF16)
-        shifted[2 * width :, :] = jnp.where(lanes == 0, low_edge, to_right).astype(BF16)
-        copies = []
-        for d in (1, 2, 3, 0):
-            at = pl.ds(pl.multiple_of(mp_peer[d] * width, width), width)
-            total = jnp.zeros((width, length), F32)
-            for k in range(3):
-                total = total + dot(turned[k, at, :], shifted[k * width : (k + 1) * width, :], NN)
-            if d == 0:
-                grad_hidden_ref[...] += total
-            else:
-                back_send[d - 1] = total.astype(BF16)
-                copies.append(
-                    send(
-                        back_send.at[d - 1], back_recv.at[d - 1], back_sems, d - 1,
-                        {"mp": mp_peer[d]},
-                    )
-                )
-        return copies
-
-    back_copies = back_convolution()
+    grad_hidden_ref[...] = grad_hidden + back(z)
     sums_a.to_far()
     sums_b.to_far()
 
-    wait(top_x_copies)
-    total = top_own[0:group, :] + top_core_recv[0:group, :].astype(F32)
-    for d in range(1, XS):
-        total = total + top_x_recv[d - 1].astype(F32)
-    top_own[0:group, :] = total
-    for p in range(1, FAR):
-        top_far_send[p - 1, 0:unit, :] = top_own[p * unit : (p + 1) * unit, :].astype(BF16)
-    top_far_copies = [
-        send(
-            top_far_send.at[p - 1], top_far_recv.at[p - 1], top_far_sems, p - 1,
-            {"seq": far_peer[p]},
-        )
-        for p in range(1, FAR)
-    ]
-
     wait(back_copies)
+    wait(gedge_copies)
     total = grad_hidden_ref[...]
+    for side, keep, at in ((0, keep_low, 0), (1, keep_high, length - 1)):
+        term = edge_recv[side, 0]
+        for k in range(1, MPS):
+            term = term + edge_recv[side, k]
+        term = (term * keep).T
+        term = jnp.concatenate([term[:, 0:1], term[0:short, 1:2]], axis=0)
+        total = total + jnp.where(lanes == at, term, 0.0)
     for d in range(1, MPS):
         total = total + back_recv[d - 1].astype(F32)
     res_skip[...] = total.astype(BF16)
@@ -544,14 +540,10 @@
         res_conv[:, k, :] = final[:, k * width : (k + 1) * width]
     final = sums_b.end()
     res_conv[:, 2, :] = final[:, 0:width]
+    res_head[...] = final[:, b_cols - tracks :]
+    stores.append(store(res_head, out_head, 2))
     stores.append(store(res_conv, out_conv, 3))
 
-    wait(top_far_copies)
-    total = top_own[0:16, :]
-    for p in range(1, FAR):
-        total = total + top_far_recv[p - 1].astype(F32)
-    res_head[...] = total[0:unit, :] * scale_back
-    stores.append(store(res_head, out_head, 2))
     wait(stores)
 
 
@@ -567,7 +559,6 @@
     half = length // 2
     group = channels // ROW
     unit = channels // SEQ
-    wide = -(-width // 128) * 128
 
     args = (
         coarse, skip, conv_weight, conv_bias.reshape(1, -1), head_weight,
@@ -601,9 +592,9 @@
     scratch = [pltpu.VMEM(a.shape, a.dtype) for k, a in enumerate(args) if k != 4]
     scratch += [
         pltpu.VMEM((MPS, width, length), BF16),
-        pltpu.VMEM((16, wide), BF16),
-        pltpu.VMEM((2, MPS, 16, wide), BF16),
-        pltpu.VMEM((MPS, 16, wide), BF16),
+        pltpu.VMEM((16, 128), BF16),
+        pltpu.VMEM((2, MPS, 16, 128), BF16),
+        pltpu.VMEM((MPS, 16, 128), BF16),
         pltpu.VMEM((MPS, width, length), BF16),
         pltpu.VMEM((channels, MPS * tracks), BF16),
         pltpu.VMEM((MPS, length, tracks), BF16),
@@ -613,7 +604,8 @@
         pltpu.VMEM((width, length), F32),
         pltpu.VMEM((width, length), F32),
         pltpu.VMEM((width, length), BF16),
-        pltpu.VMEM((2, width, half), BF16),
+        pltpu.VMEM((2, MPS, 8, 128), F32),
+        pltpu.VMEM((2, MPS, 8, 128), F32),
         pltpu.VMEM((3 * width, length), BF16),
         pltpu.VMEM((channels, channels), BF16),
         pltpu.VMEM((3, channels, length), BF16),
@@ -621,21 +613,14 @@
         pltpu.VMEM((3, channels, width), BF16),
         pltpu.VMEM((MPS - 1, width, length), BF16),
         pltpu.VMEM((MPS - 1, width, length), BF16),
-        pltpu.VMEM((channels // 2, tracks), F32),
-        pltpu.VMEM((channels // 2, tracks), BF16),
-        pltpu.VMEM((channels // 2, tracks), BF16),
-        pltpu.VMEM((XS - 1, group, tracks), BF16),
-        pltpu.VMEM((XS - 1, group, tracks), BF16),
-        pltpu.VMEM((FAR - 1, 16, tracks), BF16),
-        pltpu.VMEM((FAR - 1, 16, tracks), BF16),
         *sums(2 * width),
-        *sums(width),
+        *sums(-(-width // 128) * 128 + tracks),
         *(pltpu.VMEM(a.shape, a.dtype) for a in shapes),
         pltpu.SemaphoreType.DMA((len(args),)),
         pltpu.SemaphoreType.DMA((len(shapes),)),
         sems(2 * MPS), sems(MPS - 1), sems(2 * MPS - 2), sems(2 * MPS - 2), sems(MPS - 1),
         sems(ROW - 1), sems(MPS - 1), sems(ROW - 1), sems(MPS - 1), sems(ROW - 1),
-        sems(2), sems(MPS - 1), sems(1), sems(XS - 1), sems(FAR - 1),
+        sems(2 * MPS), sems(MPS - 1),
         sems(1), sems(XS - 1), sems(FAR - 1), sems(1), sems(XS - 1), sems(FAR - 1),
     ]
     vmem = pl.BlockSpec(memory_space=pltpu.VMEM)

time: 72.1 us -> 69 us (0.957)
  Pallas kernels: 70.6 us -> 67.7 us
    pallas_call x1, Pallas kernels: 69 us -> 66.1 us  [shards(): pl.pallas_call(body, out_shape=shapes, in_specs=[hbm] * len(args), out_sp...]
where the time goes in v4:
time: 69 us; the launch traced here: 68.3 us
  Pallas kernels  67.7 us (98%)
    pallas_call x1, Pallas kernels, shards(): pl.pallas_call(body, out_shape=shapes, in_specs=[hbm] * len(args), out_sp...  66.1 us
    pallas_call x1, Pallas kernels, shards(): pl.pallas_call(write_out, out_shape=shapes, in_specs=[vmem] * len(shapes)...  1.6 us

profile of v4, /device:TPU:1, one launch (start us, length us, event | category | flops | bytes accessed | tf_op | source)
XLA Modules:
  0.0 68.3 jit_solution(5374283696688268514)
XLA Ops:
  0.6 66.1 %shard_map.111 = (bf16[192,256]{1,0:T(8,128)(2,1)}, bf16[192,128]{1,0:T(8,128)(2,1)}, f32[6,128]{1,0:T(8,128)}, f32[6,3,192]{2,1,0:T(4,128)}) custom-call(bf16[192,128]{1,0:T(8,128)(2,1)} %coarse_in.1, bf16[192,256]{1,0:T(8,128)(2,1)} %skip_in.1, bf16[3,192,768]{2,1,0:T(8,128)(2,1)} %weight_in.1, f32[1,192]{1,0:T(1,128)} %bitcast.2, ...), custom_call_target="tpu_custom_call" | custom-call | tf_op jit(solution)/shard_map/pallas_call | solution.py:628
  66.8 1.6 %shard_map.112 = (bf16[192,256]{1,0:T(8,128)(2,1)}, bf16[192,128]{1,0:T(8,128)(2,1)}, f32[6,128]{1,0:T(8,128)}, f32[6,3,192]{2,1,0:T(4,128)}) custom-call(bf16[192,256]{1,0:T(8,128)(2,1)} %get-tuple-element.8.refs_0_, bf16[192,128]{1,0:T(8,128)(2,1)} %get-tuple-element.9.refs_1_, f32[6,128]{1,0:T(8,128)} %get-tuple-element.10.refs_2_, ...), custom_call_target="tpu_custom_call" | custom-call | tf_op jit(solution)/shard_map/pallas_call | solution.py:638

commit v5 on v4

--- a/solution.py
+++ b/solution.py
@@ -118,20 +118,24 @@
     greeted = [{"mp": p} for p in mp_peer[1:]]
     greeted += [{"seq": p, "mp": q} for p in (left, right) for q in mp_peer]
     greeted += [{"seq": p} for p in row_peer[1:] + far_peer[1:]]
+    loads = []
+
+    def load(pairs):
+        for src, dst in pairs:
+            copy = pltpu.make_async_copy(src, dst, in_sems.at[len(loads)])
+            copy.start()
+            loads.append(copy)
+
+    load(((coarse_in, coarse), (skip_in, skip)))
     for device in greeted:
         pl.semaphore_signal(barrier, inc=1, device_id=device, device_id_type=MESH)
-
-    loads = []
-    for slot, (src, dst) in enumerate(
+    load(
         (
-            (coarse_in, coarse), (skip_in, skip), (head_in, head_wide.at[:, pl.ds(0, tracks)]),
-            (counts_in, counts), (weight_in, weight), (conv_bias_in, conv_bias),
-            (head_bias_in, head_bias), (seg_mask_in, seg_mask),
-        )
-    ):
-        copy = pltpu.make_async_copy(src, dst, in_sems.at[slot])
-        copy.start()
-        loads.append(copy)
+            (head_in, head_wide.at[:, pl.ds(0, tracks)]), (counts_in, counts),
+            (weight_in, weight), (conv_bias_in, conv_bias), (head_bias_in, head_bias),
+            (seg_mask_in, seg_mask),
+        )
+    )
 
     spread = one_hot(iota((half, length), 1) // 2 == iota((half, length), 0))
     wait(loads[:2])
@@ -242,17 +246,12 @@
 
     wait(edge_copies)
     wait(mid_copies)
-    at_row, at_lane = iota((128, channels), 0), iota((128, channels), 1)
-
     def unpack(ref):
-        first = jnp.zeros((16, channels), F32)
-        second = jnp.zeros((16, channels), F32)
+        parts = []
         for k in range(MPS):
-            placed = one_hot(at_lane == at_row + k * width)
-            first = first + dot(ref[k], placed, NN)
-            placed = one_hot((at_lane == at_row + (k * width + 128)) & (at_row < short))
-            second = second + dot(ref[k], placed, NN)
-        return first + pltpu.roll(second, 15, 0)
+            tile = ref[k].astype(F32)
+            parts += [tile, pltpu.roll(tile, 15, 0)[:, 0:short]]
+        return jnp.concatenate(parts, axis=1)
 
     low_rows = unpack(edge_all.at[0])
     high_rows = unpack(edge_all.at[1])
@@ -329,16 +328,13 @@
             lanes_group == length - 1, high_edge, pltpu.roll(picked, length - 1, 1)
         ).astype(BF16)
 
-    for copy in hidden_low + hidden_high:
-        copy.wait_send()
+    wait(small_copies)
+    wait(spread_copies)
+    wait(hidden_low + hidden_high)
     counts_copies = [
         send(counts_all.at[0], counts_all.at[MPS - d], counts_sems, d - 1, {"mp": mp_peer[d]})
         for d in range(1, MPS)
     ]
-    wait(small_copies)
-    wait(spread_copies)
-    for copy in hidden_low + hidden_high:
-        copy.wait_recv()
     hidden_full = hidden_all[...].reshape(channels, length)
     products = dot(hidden_full, head_wide[...], TN)
     sigmoids, inverses = [], []

time: 69 us -> 68 us (0.986)
  no operation moved by 1% of the time
where the time goes in v5:
time: 68 us; the launch traced here: 67.8 us
  Pallas kernels  67.1 us (99%)
    pallas_call x1, Pallas kernels, shards(): pl.pallas_call(body, out_shape=shapes, in_specs=[hbm] * len(args), out_sp...  65.6 us
    pallas_call x1, Pallas kernels, shards(): pl.pallas_call(write_out, out_shape=shapes, in_specs=[vmem] * len(shapes)...  1.6 us

profile of v5, /device:TPU:1, one launch (start us, length us, event | category | flops | bytes accessed | tf_op | source)
XLA Modules:
  0.0 67.8 jit_solution(8296054455910344074)
XLA Ops:
  0.6 65.6 %shard_map.111 = (bf16[192,256]{1,0:T(8,128)(2,1)}, bf16[192,128]{1,0:T(8,128)(2,1)}, f32[6,128]{1,0:T(8,128)}, f32[6,3,192]{2,1,0:T(4,128)}) custom-call(bf16[192,128]{1,0:T(8,128)(2,1)} %coarse_in.1, bf16[192,256]{1,0:T(8,128)(2,1)} %skip_in.1, bf16[3,192,768]{2,1,0:T(8,128)(2,1)} %weight_in.1, f32[1,192]{1,0:T(1,128)} %bitcast.2, ...), custom_call_target="tpu_custom_call" | custom-call | tf_op jit(solution)/shard_map/pallas_call | solution.py:624
  66.2 1.6 %shard_map.112 = (bf16[192,256]{1,0:T(8,128)(2,1)}, bf16[192,128]{1,0:T(8,128)(2,1)}, f32[6,128]{1,0:T(8,128)}, f32[6,3,192]{2,1,0:T(4,128)}) custom-call(bf16[192,256]{1,0:T(8,128)(2,1)} %get-tuple-element.8.refs_0_, bf16[192,128]{1,0:T(8,128)(2,1)} %get-tuple-element.9.refs_1_, f32[6,128]{1,0:T(8,128)} %get-tuple-element.10.refs_2_, ...), custom_call_target="tpu_custom_call" | custom-call | tf_op jit(solution)/shard_map/pallas_call | solution.py:634

commit v6 on v5

--- a/solution.py
+++ b/solution.py
@@ -459,6 +459,16 @@
 
     for_sibling(a_core_send, (0, 1))
     sums_a.to_core()
+    for_sibling(b_core_send, (2,))
+    b_core_send[:, b_cols - tracks :] = dot(
+        hidden_pick[channels // 2 :, :], grad_logits, NN
+    ).astype(BF16)
+    sums_b.to_core()
+    for_own(a_own, (0, 1))
+    sums_a.to_x()
+    for_own(b_own, (2,))
+    b_own[:, b_cols - tracks :] = dot(hidden_pick[: channels // 2, :], grad_logits, NN)
+    sums_b.to_x()
     gb_ends = dot(ends[0], gb, NT).astype(BF16)
     for side, tap, at in ((0, 2, 2), (1, 0, 0)):
         term = dot(gb_ends, weight[tap], NN)
@@ -474,11 +484,6 @@
                     side * MPS + d, {"seq": neighbour, "mp": mp_peer[d]},
                 )
             )
-    for_sibling(b_core_send, (2,))
-    b_core_send[:, b_cols - tracks :] = dot(
-        hidden_pick[channels // 2 :, :], grad_logits, NN
-    ).astype(BF16)
-    sums_b.to_core()
     lanes = iota((width, length), 1)
     gb_wide = gb.astype(F32)
     shifted[0:width, :] = jnp.where(
@@ -500,11 +505,6 @@
         back_copies.append(
             send(back_send.at[d - 1], back_recv.at[d - 1], back_sems, d - 1, {"mp": mp_peer[d]})
         )
-    for_own(a_own, (0, 1))
-    sums_a.to_x()
-    for_own(b_own, (2,))
-    b_own[:, b_cols - tracks :] = dot(hidden_pick[: channels // 2, :], grad_logits, NN)
-    sums_b.to_x()
     grad_hidden_ref[...] = grad_hidden + back(z)
     sums_a.to_far()
     sums_b.to_far()

time: 68 us -> 69.7 us (1.025); the launches traced: 67.8 us -> 68.7 us
  Pallas kernels: 67.1 us -> 68 us
    pallas_call x1, Pallas kernels: 65.6 us -> 66.4 us  [shards(): pl.pallas_call(body, out_shape=shapes, in_specs=[hbm] * len(args), out_sp...]
where the time goes in v6:
time: 69.7 us; the launch traced here: 68.7 us
  Pallas kernels  68 us (98%)
    pallas_call x1, Pallas kernels, shards(): pl.pallas_call(body, out_shape=shapes, in_specs=[hbm] * len(args), out_sp...  66.4 us
    pallas_call x1, Pallas kernels, shards(): pl.pallas_call(write_out, out_shape=shapes, in_specs=[vmem] * len(shapes)...  1.6 us

profile of v6, /device:TPU:1, one launch (start us, length us, event | category | flops | bytes accessed | tf_op | source)
XLA Modules:
  0.0 68.7 jit_solution(5617633375022714924)
XLA Ops:
  0.6 66.4 %shard_map.111 = (bf16[192,256]{1,0:T(8,128)(2,1)}, bf16[192,128]{1,0:T(8,128)(2,1)}, f32[6,128]{1,0:T(8,128)}, f32[6,3,192]{2,1,0:T(4,128)}) custom-call(bf16[192,128]{1,0:T(8,128)(2,1)} %coarse_in.1, bf16[192,256]{1,0:T(8,128)(2,1)} %skip_in.1, bf16[3,192,768]{2,1,0:T(8,128)(2,1)} %weight_in.1, f32[1,192]{1,0:T(1,128)} %bitcast.2, ...), custom_call_target="tpu_custom_call" | custom-call | tf_op jit(solution)/shard_map/pallas_call | solution.py:624
  67.1 1.6 %shard_map.112 = (bf16[192,256]{1,0:T(8,128)(2,1)}, bf16[192,128]{1,0:T(8,128)(2,1)}, f32[6,128]{1,0:T(8,128)}, f32[6,3,192]{2,1,0:T(4,128)}) custom-call(bf16[192,256]{1,0:T(8,128)(2,1)} %get-tuple-element.8.refs_0_, bf16[192,128]{1,0:T(8,128)(2,1)} %get-tuple-element.9.refs_1_, f32[6,128]{1,0:T(8,128)} %get-tuple-element.10.refs_2_, ...), custom_call_target="tpu_custom_call" | custom-call | tf_op jit(solution)/shard_map/pallas_call | solution.py:634
